TPU v7x, 32 devices: a whole 2x2x4 slice. The times are simulated.
32 devices in a mesh: section: 2 (over core), dp: 16 (over z, y, x).
Axes of the slice: x: 2, y: 2, z: 4, core: 2. Of those that a mesh axis runs over, the one named last changes fastest.
Arguments:
- hidden_in: bfloat16 [2, 16, 128, 768], P(None, 'dp'), may hold values from -6 to 6
- out_grad: bfloat16 [2, 16, 128, 768], P(None, 'dp'), may hold values from -6 to 6
- lengths: int32 [2, 16], P(None, 'dp'), may hold values from 32 to 128, as said below
- gain_mixer: bfloat16 [2, 768], P('section', 'dp'), may hold values from 0.5 to 1.5
- w_input: bfloat16 [2, 768, 2304], P('section', 'dp'), may hold values from -0.21875 to 0.21875
- w_taps: bfloat16 [2, 3, 768], P('section', None, 'dp'), may hold values from -0.3125 to 0.3125
- filters: bfloat16 [2, 128, 768], P('section', None, 'dp'), may hold values from -0.5 to 0.5
- w_output: bfloat16 [2, 768, 768], P('section', 'dp'), may hold values from -0.21875 to 0.21875
- gain_mlp: bfloat16 [2, 768], P('section', 'dp'), may hold values from 0.5 to 1.5
- w_gate_up: bfloat16 [2, 768, 6144], P('section', 'dp'), may hold values from -0.21875 to 0.21875
- w_down: bfloat16 [2, 3072, 768], P('section', None, 'dp'), may hold values from -0.109375 to 0.109375
Outputs:
- layer_out: bfloat16 [2, 2, 16, 128, 768], P('section', None, 'dp')
- input_grad: bfloat16 [2, 2, 16, 128, 768], P('section', None, 'dp')
- grad_gain_mixer: float32 [2, 768], P('section', 'dp')
- grad_w_input: float32 [2, 768, 2304], P('section', 'dp')
- grad_w_taps: float32 [2, 3, 768], P('section', None, 'dp')
- grad_filters: float32 [2, 128, 768], P('section', None, 'dp')
- grad_w_output: float32 [2, 768, 768], P('section', 'dp')
- grad_gain_mlp: float32 [2, 768], P('section', 'dp')
- gate_up_weight_gradient: float32 [2, 768, 6144], P('section', 'dp')
- grad_w_down: float32 [2, 3072, 768], P('section', None, 'dp')
Inputs may be any that keep to these rules, and one draw needn't show every extreme that they name: `lengths`: each entry is 32, 64 or 128; some entry equals 128.
All inputs are finite; a program needn't handle non-finite values.
Results may differ from a plain program's by a relative error of at most 0.02.
Values may be sent and summed in bfloat16 or wider, within the bound.
A program may use at most 192 MiB of HBM per device.

v0:
```python
import math

import jax
import jax.numpy as jnp
from jax import lax
from jax.sharding import PartitionSpec as P

epsilon = 1e-05


def passed_along(value, axis, steps):
    count = lax.axis_size(axis)
    first, last = (max(0, -steps), min(count, count - steps))
    return lax.ppermute(value, axis, [(source, source + steps) for source in range(first, last)])


def split_dot(left_side, right_side):
    return jnp.dot(
        left_side, right_side, precision=lax.Precision.HIGH, preferred_element_type=jnp.float32
    )


def split_rows(left_side, right_side):
    return lax.dot_general(
        left_side,
        right_side,
        (((0,), (0,)), ((), ())),
        precision=lax.Precision.HIGH,
        preferred_element_type=jnp.float32,
    )


def dot_rows(left_side, right_side):
    return lax.dot_general(
        left_side, right_side, (((0,), (0,)), ((), ())), preferred_element_type=jnp.float32
    )


def dot_back(left_side, right_side):
    return lax.dot_general(
        left_side, right_side, (((1,), (1,)), ((), ())), preferred_element_type=jnp.float32
    )


def tables(length):
    period = 2 * length
    freq_index = lax.broadcasted_iota(jnp.int32, (length + 1, length), 0)
    time_index = lax.broadcasted_iota(jnp.int32, (length + 1, length), 1)
    angles = (freq_index * time_index % period).astype(jnp.float32) * (2.0 * math.pi / period)
    edge_rows = (freq_index[:, :1] == 0) | (freq_index[:, :1] == length)
    inverse_weight = jnp.where(edge_rows, 1.0, 2.0) / period
    dft_stack = jnp.concatenate([jnp.cos(angles), -jnp.sin(angles)], axis=0)
    return (dft_stack, inverse_weight)


def spectrum(dft_tables, signal):
    dft_stack, inverse_weight = dft_tables
    stacked_out = split_dot(dft_stack, signal)
    middle_row = stacked_out.shape[0] // 2
    return (stacked_out[:middle_row], stacked_out[middle_row:])


def inverse(dft_tables, real_part, imag_part):
    dft_stack, inverse_weight = dft_tables
    return split_rows(
        dft_stack, jnp.concatenate([inverse_weight * real_part, inverse_weight * imag_part], axis=0)
    )


def normalize(input_rows):
    centered = input_rows - jnp.mean(input_rows, axis=1, keepdims=True)
    inv_scale = lax.rsqrt(jnp.mean(centered * centered, axis=1, keepdims=True) + epsilon)
    return (centered * inv_scale, inv_scale)


def norm_back(grad_normed, normed, inv_scale):
    return inv_scale * (
        grad_normed
        - jnp.mean(grad_normed, axis=1, keepdims=True)
        - normed * jnp.mean(grad_normed * normed, axis=1, keepdims=True)
    )


def delayed(input_rows, places):
    return jnp.pad(input_rows, ((places, 0), (0, 0)))[: input_rows.shape[0]]


def advanced(input_rows, places):
    return jnp.pad(input_rows, ((0, places), (0, 0)))[places:]


def layer_forward(input_rows, active_rows, weights, dft_tables):
    gain_one, w_inner, w_tap_rows, filt_static, w_outer, gain_two, w_expand, w_reduce = weights
    hidden_size_model = w_outer.shape[0]
    hidden_width = w_reduce.shape[0]
    tap_weights = w_tap_rows.astype(jnp.float32)
    normed_one, scale_one = normalize(input_rows)
    entered = (normed_one * gain_one.astype(jnp.float32)).astype(jnp.bfloat16)
    projected = jnp.dot(entered, w_inner, preferred_element_type=jnp.float32)
    queries = projected[:, :hidden_size_model]
    keys_part = projected[:, hidden_size_model : 2 * hidden_size_model] * active_rows
    values_part = projected[:, 2 * hidden_size_model :] * active_rows
    dynamic = (
        tap_weights[0] * keys_part
        + tap_weights[1] * delayed(keys_part, 1)
        + tap_weights[2] * delayed(keys_part, 2)
    )
    kernel = filt_static.astype(jnp.float32) + dynamic
    joint_re, joint_im = spectrum(dft_tables, jnp.concatenate([values_part, kernel], axis=1))
    value_re = joint_re[:, :hidden_size_model]
    kernel_re = joint_re[:, hidden_size_model:]
    value_im = joint_im[:, :hidden_size_model]
    kernel_im = joint_im[:, hidden_size_model:]
    convolved = inverse(
        dft_tables,
        kernel_re * value_re - kernel_im * value_im,
        kernel_re * value_im + kernel_im * value_re,
    )
    gated_rows = (queries * convolved).astype(jnp.bfloat16)
    after_mixer = input_rows + jnp.dot(gated_rows, w_outer, preferred_element_type=jnp.float32)
    normed_two, scale_two = normalize(after_mixer)
    entered_two = (normed_two * gain_two.astype(jnp.float32)).astype(jnp.bfloat16)
    expanded = jnp.dot(entered_two, w_expand, preferred_element_type=jnp.float32)
    gate_part = expanded[:, :hidden_width]
    up_part = expanded[:, hidden_width:]
    activated = (jax.nn.silu(gate_part) * up_part).astype(jnp.bfloat16)
    result = after_mixer + jnp.dot(activated, w_reduce, preferred_element_type=jnp.float32)
    stash = (
        normed_one,
        scale_one,
        entered,
        queries,
        keys_part,
        (value_re, value_im, kernel_re, kernel_im),
        convolved,
        gated_rows,
        normed_two,
        scale_two,
        entered_two,
        gate_part,
        up_part,
        activated,
    )
    return (result, stash)


def mlp_backward(received_gradient, weights, stash):
    gain_one, w_inner, w_tap_rows, filt_static, w_outer, gain_two, w_expand, w_reduce = weights
    (
        normed_one,
        scale_one,
        entered,
        queries,
        keys_part,
        spectra,
        convolved,
        gated_rows,
        normed_two,
        scale_two,
        entered_two,
        gate_part,
        up_part,
        activated,
    ) = stash
    grad_low = received_gradient.astype(jnp.bfloat16)
    grad_reduce_w = dot_rows(activated, grad_low)
    grad_act = dot_back(grad_low, w_reduce)
    sigmoid_gate = jax.nn.sigmoid(gate_part)
    grad_gate = grad_act * up_part * (sigmoid_gate * (1.0 + gate_part * (1.0 - sigmoid_gate)))
    grad_up = grad_act * (gate_part * sigmoid_gate)
    grad_expand = jnp.concatenate([grad_gate, grad_up], axis=1).astype(jnp.bfloat16)
    grad_expand_w = dot_rows(entered_two, grad_expand)
    grad_entered_two = dot_back(grad_expand, w_expand)
    grad_gain_two = jnp.sum(grad_entered_two * normed_two, axis=0)
    grad_after = received_gradient + norm_back(
        grad_entered_two * gain_two.astype(jnp.float32), normed_two, scale_two
    )
    return (grad_after, (grad_gain_two, grad_expand_w, grad_reduce_w))


def mixer_backward(grad_after, active_rows, weights, dft_tables, stash):
    gain_one, w_inner, w_tap_rows, filt_static, w_outer, gain_two, w_expand, w_reduce = weights
    (
        normed_one,
        scale_one,
        entered,
        queries,
        keys_part,
        spectra,
        convolved,
        gated_rows,
        normed_two,
        scale_two,
        entered_two,
        gate_part,
        up_part,
        activated,
    ) = stash
    value_re, value_im, kernel_re, kernel_im = spectra
    hidden_size_model = w_outer.shape[0]
    tap_weights = w_tap_rows.astype(jnp.float32)
    grad_mix_low = grad_after.astype(jnp.bfloat16)
    grad_outer_w = dot_rows(gated_rows, grad_mix_low)
    grad_gated = dot_back(grad_mix_low, w_outer)
    grad_queries = grad_gated * convolved
    grad_conv = grad_gated * queries
    grad_re, grad_im = spectrum(dft_tables, grad_conv)
    paired_re = jnp.concatenate(
        [kernel_re * grad_re + kernel_im * grad_im, value_re * grad_re + value_im * grad_im], axis=1
    )
    paired_im = jnp.concatenate(
        [kernel_re * grad_im - kernel_im * grad_re, value_re * grad_im - value_im * grad_re], axis=1
    )
    paired = inverse(dft_tables, paired_re, paired_im)
    grad_values = paired[:, :hidden_size_model] * active_rows
    grad_kernel = paired[:, hidden_size_model:]
    grad_taps = jnp.stack(
        [
            jnp.sum(grad_kernel * keys_part, axis=0),
            jnp.sum(grad_kernel * delayed(keys_part, 1), axis=0),
            jnp.sum(grad_kernel * delayed(keys_part, 2), axis=0),
        ]
    )
    grad_keys = (
        tap_weights[0] * grad_kernel
        + tap_weights[1] * advanced(grad_kernel, 1)
        + tap_weights[2] * advanced(grad_kernel, 2)
    ) * active_rows
    grad_projected = jnp.concatenate([grad_queries, grad_keys, grad_values], axis=1).astype(
        jnp.bfloat16
    )
    inner_weight_gradient = dot_rows(entered, grad_projected)
    grad_entered = dot_back(grad_projected, w_inner)
    grad_gain_one = jnp.sum(grad_entered * normed_one, axis=0)
    grad_inputs = grad_after + norm_back(
        grad_entered * gain_one.astype(jnp.float32), normed_one, scale_one
    )
    return (
        grad_inputs,
        (grad_gain_one, inner_weight_gradient, grad_taps, grad_kernel, grad_outer_w),
    )


def add_terms(received, flipped):
    return tuple(
        (
            jnp.sum(member, axis=0).T if flip else jnp.sum(member, axis=0)
            for member, flip in zip(received, flipped)
        )
    )


def on_device(
    hidden_in,
    out_grad,
    lengths,
    gain_mixer,
    w_input,
    w_taps,
    filters,
    w_output,
    gain_mlp,
    w_gate_up,
    w_down,
):
    first_section = lax.axis_index("section") == 0
    micro_count = hidden_in.shape[0]
    seq_slots = hidden_in.shape[2]
    hidden_size_model = hidden_in.shape[3]
    dft_tables = tables(seq_slots)
    positions = lax.broadcasted_iota(jnp.int32, (seq_slots, 1), 0)
    weights = (
        lax.all_gather(gain_mixer[0], "dp", axis=0, tiled=True),
        lax.all_gather(w_input[0], "dp", axis=0, tiled=True),
        lax.all_gather(w_taps[0], "dp", axis=1, tiled=True),
        lax.all_gather(filters[0], "dp", axis=1, tiled=True),
        lax.all_gather(w_output[0], "dp", axis=0, tiled=True),
        lax.all_gather(gain_mlp[0], "dp", axis=0, tiled=True),
        lax.all_gather(w_gate_up[0], "dp", axis=0, tiled=True),
        lax.all_gather(w_down[0], "dp", axis=1, tiled=True),
    )
    arriving = jnp.zeros((seq_slots, hidden_size_model), jnp.bfloat16)
    outgoing_list = []
    saved_activations = []
    for forward_step in range(micro_count + 1):
        own_index = min(forward_step, micro_count - 1)
        prior_index = max(forward_step - 1, 0)
        input_rows = jnp.where(first_section, hidden_in[own_index, 0], arriving).astype(jnp.float32)
        length_now = jnp.where(first_section, lengths[own_index, 0], lengths[prior_index, 0])
        active_rows = (positions < length_now).astype(jnp.float32)
        result, stash = layer_forward(input_rows, active_rows, weights, dft_tables)
        outgoing = result.astype(jnp.bfloat16)
        outgoing_list.append(outgoing)
        if forward_step < micro_count:
            arriving = passed_along(outgoing, "section", 1)
        saved_activations.append((input_rows, active_rows))
    coming = jnp.zeros((seq_slots, hidden_size_model), jnp.bfloat16)
    mlp_totals = None
    mixer_totals = None
    grads_out = []
    for backward_step in range(micro_count + 1):
        saved_slot_index = micro_count - backward_step
        last_index = max(micro_count - 1 - backward_step, 0)
        live_factor = 1.0 if backward_step < micro_count else 0.0
        received_gradient = jnp.where(
            first_section,
            coming.astype(jnp.float32),
            out_grad[last_index, 0].astype(jnp.float32) * live_factor,
        )
        input_rows, active_rows = saved_activations[saved_slot_index]
        result, stash = layer_forward(input_rows, active_rows, weights, dft_tables)
        grad_after, mlp_grads = mlp_backward(received_gradient, weights, stash)
        mlp_totals = (
            mlp_grads if mlp_totals is None else jax.tree.map(jnp.add, mlp_totals, mlp_grads)
        )
        grad_inputs, mixer_grads = mixer_backward(
            grad_after, active_rows, weights, dft_tables, stash
        )
        mixer_totals = (
            mixer_grads
            if mixer_totals is None
            else jax.tree.map(jnp.add, mixer_totals, mixer_grads)
        )
        outgoing = grad_inputs.astype(jnp.bfloat16)
        grads_out.append(outgoing)
        if backward_step < micro_count:
            coming = passed_along(outgoing, "section", -1)
    first_outputs = jnp.stack(outgoing_list[:micro_count])
    second_outputs = jnp.stack(outgoing_list[1:])
    layer_out = jnp.where(first_section, first_outputs, second_outputs)[None, :, None]
    first_grads = jnp.stack(
        [grads_out[micro_count - batch_index] for batch_index in range(micro_count)]
    )
    second_grads = jnp.stack(
        [grads_out[micro_count - 1 - batch_index] for batch_index in range(micro_count)]
    )
    input_grad = jnp.where(first_section, first_grads, second_grads)[None, :, None]
    all_parts = (
        lax.all_to_all(
            mixer_totals[0][None].astype(jnp.bfloat16),
            "dp",
            split_axis=1,
            concat_axis=0,
            tiled=True,
        ).astype(jnp.float32),
        lax.all_to_all(
            mixer_totals[1][None].astype(jnp.bfloat16),
            "dp",
            split_axis=1,
            concat_axis=0,
            tiled=True,
        ).astype(jnp.float32),
        lax.all_to_all(
            mixer_totals[2].T[None].astype(jnp.bfloat16),
            "dp",
            split_axis=1,
            concat_axis=0,
            tiled=True,
        ).astype(jnp.float32),
        lax.all_to_all(
            mixer_totals[3].T[None].astype(jnp.bfloat16),
            "dp",
            split_axis=1,
            concat_axis=0,
            tiled=True,
        ).astype(jnp.float32),
        lax.all_to_all(
            mixer_totals[4][None].astype(jnp.bfloat16),
            "dp",
            split_axis=1,
            concat_axis=0,
            tiled=True,
        ).astype(jnp.float32),
        lax.all_to_all(
            mlp_totals[0][None].astype(jnp.bfloat16), "dp", split_axis=1, concat_axis=0, tiled=True
        ).astype(jnp.float32),
        lax.all_to_all(
            mlp_totals[1][None].astype(jnp.bfloat16), "dp", split_axis=1, concat_axis=0, tiled=True
        ).astype(jnp.float32),
        lax.all_to_all(
            mlp_totals[2].T[None].astype(jnp.bfloat16),
            "dp",
            split_axis=1,
            concat_axis=0,
            tiled=True,
        ).astype(jnp.float32),
    )
    summed = add_terms(all_parts, (False, False, True, True, False, False, False, True))
    return (
        layer_out,
        input_grad,
        summed[0][None],
        summed[1][None],
        summed[2][None],
        summed[3][None],
        summed[4][None],
        summed[5][None],
        summed[6][None],
        summed[7][None],
    )


def solution(mesh):
    placed = (
        P(None, "dp", None, None),
        P(None, "dp", None, None),
        P(None, "dp"),
        P("section", "dp"),
        P("section", "dp", None),
        P("section", None, "dp"),
        P("section", None, "dp"),
        P("section", "dp", None),
        P("section", "dp"),
        P("section", "dp", None),
        P("section", None, "dp"),
    )
    return jax.shard_map(
        on_device,
        mesh=mesh,
        in_specs=placed,
        out_specs=(
            P("section", None, "dp", None, None),
            P("section", None, "dp", None, None),
            P("section", "dp"),
            P("section", "dp", None),
            P("section", None, "dp"),
            P("section", None, "dp"),
            P("section", "dp", None),
            P("section", "dp"),
            P("section", "dp", None),
            P("section", None, "dp"),
        ),
        check_vma=False,
    )
```

profile of v0, /device:TPU:28, one launch (start us, length us, event | category | flops | bytes accessed | tf_op | source)
XLA Modules:
  0.0 1089.9 jit_solution(15239433408877930776)
XLA Ops:
  13.6 35.9 %all-reduce.14 = (bf16[768]{0:T(1024)(128)(2,1)S(1)}, bf16[768]{0:T(1024)(128)(2,1)S(1)}) all-reduce(bf16[768]{0:T(1024)(128)(2,1)S(1)} %dynamic-update-slice, bf16[768]{0:T(1024)(128)(2,1)S(1)} %dynamic-update-slice.1), channel_id=2, replica_groups=mesh['section'=2,'dp'=16] {'dp'}, use_global_device_ids=true, to_apply=%add.12 | all-reduce | flops 1536 | bytes 6144
  50.3 40.1 %all-gather.2 = bf16[1,128,768]{1,2,0:T(8,128)(2,1)S(1)} all-gather(bf16[1,128,48]{1,2,0:T(8,128)(2,1)} %param.17), channel_id=4, replica_groups=mesh['section'=2,'dp'=16] {'dp'}, dimensions={2}, use_global_device_ids=true | all-gather | bytes 208896 | tf_op jit(solution)/shard_map/all_gather | solution.py:276
  90.6 38.1 %all-gather.3 = bf16[1,3,768]{1,0,2:T(2,128)(2,1)S(1)} all-gather(bf16[1,3,48]{1,0,2:T(2,128)(2,1)S(1)} %copy.46), channel_id=5, replica_groups=mesh['section'=2,'dp'=16] {'dp'}, dimensions={2}, use_global_device_ids=true | all-gather | bytes 4896 | tf_op jit(solution)/shard_map/all_gather | solution.py:275
  131.1 7.6 slice_reduce_fusion.2
  147.8 117.8 %all-gather.17.cloned.1.call-done = bf16[1,768,6144]{2,1,0:T(8,128)(2,1)} async-done(((bf16[1,48,6144]{2,1,0:T(8,128)(2,1)}), bf16[1,768,6144]{2,1,0:T(8,128)(2,1)}) %all-gather.17.cloned.1.call-update) | async-done | bytes 9437200 | tf_op jit(solution)/shard_map/all_gather | solution.py:279
  273.6 73.8 %all-gather.19.cloned.1.call-done = bf16[1,3072,768]{1,2,0:T(8,128)(2,1)} async-done(((bf16[1,3072,48]{1,2,0:T(8,128)(2,1)}), bf16[1,3072,768]{1,2,0:T(8,128)(2,1)}) %all-gather.19.cloned.1.call-update) | async-done | bytes 4718608 | tf_op jit(solution)/shard_map/all_gather | solution.py:280
  449.1 6.9 all-to-all-start
  459.2 8.1 all-to-all-start.2
  477.1 6.9 all-to-all-start.3
  486.8 7.8 reduce.13
  495.9 7.6 all-to-all-start.4
  507.4 20.7 %copy.67 = bf16[1,768,2304]{2,0,1:T(2,128)(2,1)} copy(bf16[1,768,2304]{2,1,0:T(8,128)(2,1)S(1)} %fusion.25) | data formatting | bytes 7077888 | tf_op jit(solution)/shard_map/convert_element_type | solution.py:347
  528.2 75.2 %reduce.11 = bf16[768,2304]{1,0:T(8,128)(2,1)S(1)} reduce(bf16[768,1,2304]{2,1,0:T(2,128)(2,1)} %bitcast.257, bf16[]{:T(256)} %broadcast.347), dimensions={1}, to_apply=%bitcast.243.reduce_sub_computation | reduce | bytes 7077890
  609.5 7.4 all-to-all-start.1
  623.5 9.7 copy.66
  633.1 28.9 %reduce.15 = bf16[768,3072]{1,0:T(8,128)(2,1)} reduce(bf16[768,1,3072]{2,1,0:T(2,128)(2,1)} %bitcast.252, bf16[]{:T(256)} %broadcast.347), dimensions={1}, to_apply=%bitcast.242.reduce_sub_computation | reduce | bytes 9437186
  662.1 11.8 %reshape.466 = bf16[16,2,73728]{2,1,0:T(2,128)(2,1)} reshape(bf16[768,3072]{1,0:T(8,128)(2,1)} %reduce.15) | data formatting | bytes 9437184
  673.9 18.4 %all-to-all-done.1 = bf16[16,2,55296]{2,1,0:T(2,128)(2,1)} async-done(((bf16[16,2,55296]{2,1,0:T(2,128)(2,1)}), bf16[16,2,55296]{2,1,0:T(2,128)(2,1)}, u32[]{:S(2)}, u32[]{:S(2)}) %all-to-all-start.1) | async-done | bytes 3538976 | tf_op jit(solution)/shard_map/all_to_all | solution.py:346
  698.8 8.0 fusion.86
  706.9 8.2 fusion.85
  715.1 17.2 %fusion.12 = bf16[1,768,6144]{2,1,0:T(8,128)(2,1)} fusion(f32[768,6144]{1,0:T(8,128)} %fusion.86, f32[768,6144]{1,0:T(8,128)} %fusion.85, bf16[128,3072]{1,0:T(8,128)(2,1)S(1)} %copy-done.101, bf16[128,3072]{1,0:T(8,128)(2,1)S(1)} %copy-done.99, f32[128,768]{1,0:T(8,128)S(1)} %copy-done.4, f32[768]{0:T(1024)S(1)} %convert_element_type.438, ...), kind=kOutput, calls=%fused_computation.14 | convolution fusion | flops 1225654272 | bytes 49156096 | tf_op jit(solution)/shard_map/dot_general | solution.py:34
  732.3 17.5 %copy.65 = bf16[1,768,6144]{2,0,1:T(2,128)(2,1)} copy(bf16[1,768,6144]{2,1,0:T(8,128)(2,1)} %fusion.12) | data formatting | bytes 18874368 | tf_op jit(solution)/shard_map/convert_element_type | solution.py:378
  749.8 57.3 %reduce.14 = bf16[768,6144]{1,0:T(8,128)(2,1)} reduce(bf16[768,1,6144]{2,1,0:T(2,128)(2,1)} %bitcast.249, bf16[]{:T(256)} %broadcast.347), dimensions={1}, to_apply=%bitcast.241.reduce_sub_computation | reduce | bytes 18874370
  807.0 15.2 %reshape.464 = bf16[16,2,147456]{2,1,0:T(2,128)(2,1)} reshape(bf16[768,6144]{1,0:T(8,128)(2,1)} %reduce.14) | data formatting | bytes 18874368
  822.3 7.3 all-to-all-start.6
  851.2 11.9 %reshape.459 = bf16[768,1,2304]{2,1,0:T(2,128)(2,1)} reshape(bf16[16,2,55296]{2,1,0:T(2,128)(2,1)} %all-to-all-done.1) | data formatting | bytes 7077888
  873.5 12.8 %reshape.467 = bf16[768,1,3072]{2,1,0:T(2,128)(2,1)} reshape(bf16[16,2,73728]{2,1,0:T(2,128)(2,1)} %all-to-all-done.7) | data formatting | bytes 9437184
  886.4 9.6 copy.60
  901.0 138.4 %all-to-all-done.6 = bf16[16,2,147456]{2,1,0:T(2,128)(2,1)} async-done(((bf16[16,2,147456]{2,1,0:T(2,128)(2,1)}), bf16[16,2,147456]{2,1,0:T(2,128)(2,1)}, u32[]{:S(2)}, u32[]{:S(2)}) %all-to-all-start.6) | async-done | bytes 9437216 | tf_op jit(solution)/shard_map/all_to_all | solution.py:377
  1039.4 17.4 %reshape.465 = bf16[768,1,6144]{2,1,0:T(2,128)(2,1)} reshape(bf16[16,2,147456]{2,1,0:T(2,128)(2,1)} %all-to-all-done.6) | data formatting | bytes 18874368
  1056.9 17.6 %copy.59 = f32[1,768,6144]{2,1,0:T(8,128)} copy(bf16[1,768,6144]{2,0,1:T(2,128)(2,1)} %bitcast.248) | data formatting | bytes 28311552
  1074.5 8.4 reduce_sum.516
  (482 shorter events, 201.6 us)
Async XLA Ops:
  7.2 121.9 %copy-start.137 = (s32[2,1]{0,1:T(1,128)S(1)}, s32[2,1]{0,1:T(1,128)}, u32[]{:S(2)}) copy-start(s32[2,1]{0,1:T(1,128)} %param.13) | copy-start | bytes 28
  7.2 123.5 %copy-start.31 = (bf16[2,1,128,768]{3,2,1,0:T(8,128)(2,1)S(1)}, bf16[2,1,128,768]{3,2,1,0:T(8,128)(2,1)}, u32[]{:S(2)}) copy-start(bf16[2,1,128,768]{3,2,1,0:T(8,128)(2,1)} %param.11) | copy-start | bytes 1179652
  7.2 131.5 %all-gather.13.cloned.1.call-start = ((), (), s32[]{:S(2)}) async-start(), calls=%async_computation.8 | async-start | bytes 3760128 | tf_op jit(solution)/shard_map/all_gather | solution.py:274
  7.9 136.1 %all-gather.15.cloned.1.call-start = ((), (), s32[]{:S(2)}) async-start(), calls=%async_computation.9 | async-start | bytes 1253376 | tf_op jit(solution)/shard_map/all_gather | solution.py:277
  8.7 256.9 %all-gather.17.cloned.1.call-start = ((), (), s32[]{:S(2)}) async-start(), calls=%async_computation.10 | async-start | bytes 10027008 | tf_op jit(solution)/shard_map/all_gather | solution.py:279
  9.4 338.0 %all-gather.19.cloned.1.call-start = ((), (), s32[]{:S(2)}) async-start(), calls=%async_computation.11 | async-start | bytes 5013504 | tf_op jit(solution)/shard_map/all_gather | solution.py:280
  130.7 297.3 %copy-start.17 = (f32[129,128]{1,0:T(8,128)}, f32[129,128]{1,0:T(8,128)S(1)}, u32[]{:S(2)}) copy-start(f32[129,128]{1,0:T(8,128)S(1)} %get-tuple-element.116) | copy-start | bytes 198148
  130.7 297.3 %copy-start.19 = (f32[129,128]{1,0:T(8,128)}, f32[129,128]{1,0:T(8,128)S(1)}, u32[]{:S(2)}) copy-start(f32[129,128]{1,0:T(8,128)S(1)} %get-tuple-element.117) | copy-start | bytes 198148
  138.6 275.2 %copy-start.103 = (f32[768]{0:T(1024)}, f32[768]{0:T(1024)S(1)}, u32[]{:S(2)}) copy-start(f32[768]{0:T(1024)S(1)} %get-tuple-element.39) | copy-start | bytes 9220
  144.0 126.7 %copy-start.59 = (bf16[128,768]{1,0:T(8,128)(2,1)}, bf16[128,768]{1,0:T(8,128)(2,1)S(1)}, u32[]{:S(2)}) copy-start(bf16[128,768]{1,0:T(8,128)(2,1)S(1)} %get-tuple-element.92) | copy-start | bytes 589828
  145.8 280.0 %copy-start.3 = (f32[128,768]{1,0:T(8,128)}, f32[128,768]{1,0:T(8,128)S(1)}, u32[]{:S(2)}) copy-start(f32[128,768]{1,0:T(8,128)S(1)} %get-tuple-element.95) | copy-start | bytes 1179652
  352.6 3.8 collective-permute-start
  357.4 59.0 %copy-start.21 = (bf16[128,768]{1,0:T(8,128)(2,1)}, bf16[128,768]{1,0:T(8,128)(2,1)S(1)}, u32[]{:S(2)}) copy-start(bf16[128,768]{1,0:T(8,128)(2,1)S(1)} %get-tuple-element.45) | copy-start | bytes 589828
  357.5 59.0 %copy-start.115 = (f32[128]{0:T(128)}, f32[128]{0:T(128)S(1)}, u32[]{:S(2)}) copy-start(f32[128]{0:T(128)S(1)} %broadcast_multiply_fusion.15) | copy-start | bytes 1540
  357.7 58.8 %copy-start.125 = (f32[128]{0:T(128)}, f32[128]{0:T(128)S(1)}, u32[]{:S(2)}) copy-start(f32[128]{0:T(128)S(1)} %add_rsqrt_fusion.3) | copy-start | bytes 1540
  365.3 43.2 %copy-start.5 = (f32[128,768]{1,0:T(8,128)}, f32[128,768]{1,0:T(8,128)S(1)}, u32[]{:S(2)}) copy-start(f32[128,768]{1,0:T(8,128)S(1)} %get-tuple-element.99) | copy-start | bytes 1179652
  365.4 43.2 %copy-start.106 = (f32[128]{0:T(128)}, f32[128]{0:T(128)S(1)}, u32[]{:S(2)}) copy-start(f32[128]{0:T(128)S(1)} %broadcast_multiply_fusion.14) | copy-start | bytes 1540
  365.6 43.0 %copy-start.110 = (f32[128]{0:T(128)}, f32[128]{0:T(128)S(1)}, u32[]{:S(2)}) copy-start(f32[128]{0:T(128)S(1)} %add_rsqrt_fusion.2) | copy-start | bytes 1540
  371.0 2.8 collective-permute-start.1
  397.0 3.3 collective-permute-start.2
  416.7 3.3 collective-permute-start.3
  436.0 13.1 %all-to-all-start.5 = ((bf16[1,16,48]{2,0,1:T(2,128)(2,1)}), bf16[1,16,48]{2,0,1:T(2,128)(2,1)}, u32[]{:S(2)}, u32[]{:S(2)}) async-start(bf16[1,16,48]{2,0,1:T(2,128)(2,1)} %convert_element_type.440), calls=%async_computation.5 | async-start | bytes 16384 | tf_op jit(solution)/shard_map/all_to_all | solution.py:374
  449.1 10.1 all-to-all-start
  459.2 17.9 %all-to-all-start.2 = ((bf16[1,768,3]{2,0,1:T(2,128)(2,1)}), bf16[1,768,3]{2,0,1:T(2,128)(2,1)}, u32[]{:S(2)}, u32[]{:S(2)}) async-start(bf16[1,768,3]{2,0,1:T(2,128)(2,1)} %copy.49), calls=%async_computation.2 | async-start | bytes 786432 | tf_op jit(solution)/shard_map/all_to_all | solution.py:353
  477.1 18.8 %all-to-all-start.3 = ((bf16[16,2,3072]{2,1,0:T(2,128)(2,1)}), bf16[16,2,3072]{2,1,0:T(2,128)(2,1)}, u32[]{:S(2)}, u32[]{:S(2)}) async-start(bf16[16,2,3072]{2,1,0:T(2,128)(2,1)} %reshape.460), calls=%async_computation.3 | async-start | bytes 393216 | tf_op jit(solution)/shard_map/all_to_all | solution.py:360
  495.9 113.6 %all-to-all-start.4 = ((bf16[16,2,18432]{2,1,0:T(2,128)(2,1)}), bf16[16,2,18432]{2,1,0:T(2,128)(2,1)}, u32[]{:S(2)}, u32[]{:S(2)}) async-start(bf16[16,2,18432]{2,1,0:T(2,128)(2,1)} %reshape.462), calls=%async_computation.4 | async-start | bytes 2359296 | tf_op jit(solution)/shard_map/all_to_all | solution.py:367
  609.5 82.8 %all-to-all-start.1 = ((bf16[16,2,55296]{2,1,0:T(2,128)(2,1)}), bf16[16,2,55296]{2,1,0:T(2,128)(2,1)}, u32[]{:S(2)}, u32[]{:S(2)}) async-start(bf16[16,2,55296]{2,1,0:T(2,128)(2,1)} %reshape.458), calls=%async_computation.1 | async-start | bytes 7077888 | tf_op jit(solution)/shard_map/all_to_all | solution.py:346
  673.9 24.8 %copy-start.75 = (bf16[128,3072]{1,0:T(8,128)(2,1)S(1)}, bf16[128,3072]{1,0:T(8,128)(2,1)}, u32[]{:S(2)}) copy-start(bf16[128,3072]{1,0:T(8,128)(2,1)} %get-tuple-element.51) | copy-start | bytes 2359300
  673.9 24.8 %copy-start.105 = (f32[128]{0:T(128)S(1)}, f32[128]{0:T(128)}, u32[]{:S(2)}) copy-start(f32[128]{0:T(128)} %copy-done.104) | copy-start | bytes 1540
  673.9 24.9 %copy-start.109 = (f32[128]{0:T(128)S(1)}, f32[128]{0:T(128)}, u32[]{:S(2)}) copy-start(f32[128]{0:T(128)} %copy-done.108) | copy-start | bytes 1540
  692.3 129.9 %all-to-all-start.7 = ((bf16[16,2,73728]{2,1,0:T(2,128)(2,1)}), bf16[16,2,73728]{2,1,0:T(2,128)(2,1)}, u32[]{:S(2)}, u32[]{:S(2)}) async-start(bf16[16,2,73728]{2,1,0:T(2,128)(2,1)} %reshape.466), calls=%async_computation.7 | async-start | bytes 9437184 | tf_op jit(solution)/shard_map/all_to_all | solution.py:380
  822.3 217.2 %all-to-all-start.6 = ((bf16[16,2,147456]{2,1,0:T(2,128)(2,1)}), bf16[16,2,147456]{2,1,0:T(2,128)(2,1)}, u32[]{:S(2)}, u32[]{:S(2)}) async-start(bf16[16,2,147456]{2,1,0:T(2,128)(2,1)} %reshape.464), calls=%async_computation.6 | async-start | bytes 18874368 | tf_op jit(solution)/shard_map/all_to_all | solution.py:377
  (129 other events, 732.0 us)
Sparse Core Ops, SparseCore 0:
  10.8 72.0 all-gather.12
  85.7 56.3 all-gather.14
  144.9 120.6 all-gather.16
  268.2 79.1 all-gather.18
where the time goes:
time: 1100 us; the launch traced here: 1090 us
  waiting for transfers between devices  361 us (33%)
  other arithmetic  216 us (20%)
  local copies, waits for them, and re-layouts  196 us (18%)
  matrix products  120 us (11%)
  blocking collectives  114 us (10%)
  starting transfers between devices  64.4 us (6%)
  between operations  18.7 us (2%)
    unnamed x7, other arithmetic  171 us
    all_to_all x1, waiting for transfers between devices, on_device(): lax.all_to_all(mlp_totals[1][None].astype(jnp.bfloat16), 'dp', split_axis...  138 us
    unnamed x311, local copies, waits for them, and re-layouts  131 us
    all_gather x1, waiting for transfers between devices, on_device(): lax.all_gather(w_gate_up[0], 'dp', axis=0, tiled=True)  118 us
    all_gather x1, waiting for transfers between devices, on_device(): lax.all_gather(w_down[0], 'dp', axis=1, tiled=True)  73.8 us
    dot_general x12, matrix products, dot_rows(): lax.dot_general(left_side, right_side, (((0,), (0,)), ((), ())), preferre...  45 us
    all_gather x1, blocking collectives, on_device(): lax.all_gather(filters[0], 'dp', axis=1, tiled=True)  40.1 us
    all_gather x1, blocking collectives, on_device(): lax.all_gather(w_taps[0], 'dp', axis=1, tiled=True)  38.1 us
  transfers between devices with their start and end apart: 16, of which 9 were waited for; matrix products, arithmetic and copies ran while one was open for 38% of the time, Pallas kernels for 0%

commit v1 on v0

--- a/solution.py
+++ b/solution.py
@@ -1,11 +1,43 @@
+import functools
 import math
 
 import jax
 import jax.numpy as jnp
+import ml_dtypes
+import numpy as np
 from jax import lax
+from jax.experimental import pallas as pl
+from jax.experimental.pallas import tpu as pltpu
 from jax.sharding import PartitionSpec as P
 
+MESH = pl.DeviceIdType.MESH
+
 epsilon = 1e-05
+GET_PIECES = (
+    (0, 128, False),
+    (1, 384, False),
+    (1, 384, False),
+    (1, 384, False),
+    (2, 384, False),
+    (3, 1024, False),
+    (3, 1024, False),
+    (3, 1024, False),
+    (4, 512, False),
+    (4, 512, False),
+    (4, 512, False),
+)
+PUT_PIECES = (
+    (4, 768, False),
+    (4, 768, False),
+    (3, 1024, False),
+    (3, 1024, False),
+    (3, 1024, False),
+    (2, 384, False),
+    (1, 384, False),
+    (1, 384, False),
+    (1, 384, False),
+    (0, 128, False),
+)
 
 
 def passed_along(value, axis, steps):
@@ -400,6 +432,852 @@
     )
 
 
+class Place:
+    def __init__(self):
+        self.core = lax.axis_index("section")
+        self.index = lax.axis_index("dp")
+        self.z = self.index // 4
+        self.y = self.index // 2 % 2
+        self.x = self.index % 2
+        self.layer = 1 - (self.z + 1) // 2 % 2
+        self.home = self.z // 2
+        self.first_layer = self.layer == 0
+        self.second_layer = self.layer == 1
+        self.partner = self.chip(z=self.z + 1 - 2 * (self.z % 2))
+
+    def chip(self, z=None, y=None, x=None):
+        z, y, x = (a if a is not None else b for a, b in ((z, self.z), (y, self.y), (x, self.x)))
+        return z * 4 + y * 2 + x
+
+    def x_side(self):
+        return (self.core, self.chip(x=1 - self.x))
+
+    def y_side(self):
+        return (self.core, self.chip(y=1 - self.y))
+
+    def sibling(self):
+        return (1 - self.core, self.index)
+
+    def middle(self):
+        return (self.core, self.chip(z=3 - self.z))
+
+    def greet(self):
+        barrier = pltpu.get_barrier_semaphore()
+        others = [self.x_side(), self.y_side(), self.sibling()]
+        for step in (1, 2, 3):
+            chip = self.chip(z=(self.z + step) % 4)
+            others += [(0, chip), (1, chip)]
+        for other in others:
+            pl.semaphore_signal(barrier, inc=1, device_id=other, device_id_type=MESH)
+        pl.semaphore_wait(barrier, len(others))
+
+
+def remote(source, target, send, receive, device):
+    return pltpu.make_async_remote_copy(
+        src_ref=source,
+        dst_ref=target,
+        send_sem=send,
+        recv_sem=receive,
+        device_id=device,
+        device_id_type=MESH,
+    )
+
+
+def chunks_of(pieces):
+    table, places = [], {}
+    for array, width, shared in pieces:
+        start = places.get(array, 0)
+        table.append((array, start, width, shared))
+        places[array] = start + width
+    return table
+
+
+def left_dot(left_side, right_side):
+    return lax.dot_general(
+        left_side, right_side, (((1,), (0,)), ((), ())), preferred_element_type=jnp.float32
+    )
+
+
+def parts(signal):
+    high = signal.astype(jnp.bfloat16)
+    rest = (signal - high.astype(jnp.float32)).astype(jnp.bfloat16)
+    return jnp.concatenate([high, high, rest], axis=0)
+
+
+def halves_of(table):
+    high = table.astype(ml_dtypes.bfloat16)
+    rest = (table - high.astype(np.float64)).astype(ml_dtypes.bfloat16)
+    return np.concatenate([high, rest, high], axis=1)
+
+
+def packed_tables(length):
+    period = 2 * length
+    freq, time = np.arange(length)[:, None], np.arange(length)[None, :]
+    angles = (freq * time % period) * (2.0 * math.pi / period)
+    sines = np.where(freq == 0, 1.0 - 2.0 * (time % 2), -np.sin(angles))
+    table = np.concatenate([np.cos(angles), sines], axis=0)
+    weight = np.where(np.arange(period)[:, None] % length == 0, 1.0, 2.0) / period
+    return halves_of(table), halves_of((table * weight).T)
+
+
+def layer_kernel(get_table, put_table, widths, *refs):
+    refs = list(refs)
+
+    def take(number):
+        taken = refs[:number]
+        del refs[:number]
+        return taken
+
+    filters_in, taps_in, gain_one_in, gain_two_in, lengths_in, dft, idft = take(7)
+    shards, (hidden_in, grad_in) = [None] + take(4), take(2)
+    landed, (kept_out, kept_grad) = take(5), take(2)
+    own_small, rows_in, live_own, live = take(4)
+    weight = take(5)
+    feed, arrive, x_in, e_in, out_low, grad_low = take(6)
+    filt, rows8, norm_one, norm_two, scale_one, scale_two = take(6)
+    left, queries, keys, values, convolved, value_spec, kernel_spec = take(7)
+    total, after, expanded, active, projected, after_low, small_terms = take(7)
+    lefts = take(4)
+    other_small, other_projected, other_after, other_expanded, other_active = take(5)
+    mine = take(len(put_table))
+    one_small, two_small = take(2)
+    get_z_send, get_z_recv, get_one_send, get_one_recv, get_two_send, get_two_recv = take(6)
+    get_mid_send, get_mid_recv, get_side_send, get_side_recv, feed_sems = take(5)
+    swap_sems, send, recv = take(3)
+    one_send, one_recv, two_send, two_recv, z_send, z_recv, mid_send, mid_recv, ready = take(9)
+
+    here = Place()
+    tokens, features = x_in.shape
+    slots = filt.shape[0]
+    micro = tokens // slots
+    hidden = active.shape[1]
+    f32, low = jnp.float32, jnp.bfloat16
+    shards[0] = own_small
+
+    rows_in[...] = jnp.zeros_like(rows_in)
+    own = taps_in.shape[1]
+    rows_in[0:3, 0:own] = taps_in[...].astype(f32)
+    rows_in[3:4, 0:own] = gain_one_in[...].astype(f32)
+    rows_in[4:5, 0:own] = gain_two_in[...].astype(f32)
+    own_small[:, :128] = filters_in[...]
+    own_small[:, 128:] = rows_in[...].T[:own].astype(low)
+    for m in range(micro):
+        live_own[m] = jnp.full(live_own.shape[1:], lengths_in[m, 0], jnp.int32).astype(f32)
+    here.greet()
+
+    own_feed = here.core == here.layer
+    partner = (here.core, here.partner)
+    for layer, kept, given in ((0, hidden_in, grad_in), (1, grad_in, hidden_in)):
+
+        @pl.when(own_feed & (here.layer == layer))
+        def _():
+            pltpu.make_async_copy(kept, feed, feed_sems.at[0]).start()
+            pltpu.make_async_copy(live_own, live, feed_sems.at[2]).start()
+            remote(given, feed, feed_sems.at[1], feed_sems.at[0], partner).start()
+            remote(live_own, live, feed_sems.at[3], feed_sems.at[2], partner).start()
+
+    def arrived(target, receive):
+        pltpu.make_async_copy(target, target, receive).wait()
+
+    def fed():
+        arrived(feed, feed_sems.at[0])
+        arrived(live, feed_sems.at[2])
+
+    def columns(table, chunk, half):
+        array, start, width, _ = table[chunk]
+        return pl.ds(pl.multiple_of(half * (widths[array] // 2) + start, 128), width)
+
+    def at_home(z):
+        return z // 2 == here.home
+
+    def when(condition, action):
+        if condition is True:
+            action()
+        else:
+            pl.when(condition)(action)
+
+    def z_all(chunk, visit):
+        array, _, _, shared = get_table[chunk]
+        for number, plane in enumerate((1 - here.core, 2 + here.core)):
+            wanted = (here.core == 1) | (here.home == number) if shared else here.z >= 0
+            for half in (0, 1):
+                own = (plane == here.z) & (here.core == half)
+                cut = columns(get_table, chunk, half)
+                source, target = shards[array].at[:, cut], weight[array].at[here.z, here.y, here.x, :, cut]
+                sems = get_z_send.at[chunk, number, half], get_z_recv.at[chunk, here.z]
+                visit(wanted, own, source, target, sems, (half, here.chip(z=plane)))
+
+    def z_start(chunk):
+        def visit(wanted, own, source, target, sems, device):
+            @pl.when(wanted & own)
+            def _():
+                pltpu.make_async_copy(source, target, sems[1]).start()
+
+            @pl.when(wanted & jnp.logical_not(own))
+            def _():
+                remote(source, target, *sems, device).start()
+
+        z_all(chunk, visit)
+
+    def z_sent(chunk):
+        def visit(wanted, own, source, target, sems, device):
+            @pl.when(wanted & jnp.logical_not(own))
+            def _():
+                remote(source, target, *sems, device).wait_send()
+
+        z_all(chunk, visit)
+
+    def far(step):
+        return (here.z + step) % 4
+
+    def handled(table, chunk, z):
+        return here.second_layer | at_home(z) if table[chunk][3] else True
+
+    def get_first(chunk, step):
+        block = weight[get_table[chunk][0]].at[far(step), here.y, here.x, :, columns(get_table, chunk, here.core)]
+        side = here.y_side() if step % 2 else here.x_side()
+        return remote(block, block, get_one_send.at[chunk, step], get_one_recv.at[chunk, step], side)
+
+    def get_second(chunk, step):
+        ref, cut = weight[get_table[chunk][0]], columns(get_table, chunk, here.core)
+        if step % 2:
+            pair, side = ref.at[far(step), :, here.x, :, cut], here.x_side()
+        else:
+            pair, side = ref.at[far(step), here.y, :, :, cut], here.y_side()
+        return remote(pair, pair, get_two_send.at[chunk, step], get_two_recv.at[chunk, step], side)
+
+    def get_middle(chunk, z):
+        block = weight[get_table[chunk][0]].at[z, :, :, :, columns(get_table, chunk, here.core)]
+        return remote(block, block, get_mid_send.at[chunk, z % 2], get_mid_recv.at[chunk, z % 2], here.middle())
+
+    def get_across(chunk):
+        whole = weight[get_table[chunk][0]].at[:, :, :, :, columns(get_table, chunk, here.core)]
+        return remote(whole, whole, get_side_send.at[chunk], get_side_recv.at[chunk], here.sibling())
+
+    def one_step(chunk, step):
+        def action():
+            z = far(step)
+            block = weight[get_table[chunk][0]].at[z, here.y, here.x, :, columns(get_table, chunk, here.core)]
+            arrived(block, get_z_recv.at[chunk, z])
+            get_first(chunk, step).start()
+
+        when(handled(get_table, chunk, far(step)), action)
+
+    def two_steps(chunk, step):
+        def action():
+            get_first(chunk, step).wait_recv()
+            get_second(chunk, step).start()
+
+        when(handled(get_table, chunk, far(step)), action)
+
+    def three_steps(chunk, step):
+        def action():
+            get_second(chunk, step).wait_recv()
+            if get_table[chunk][3]:
+
+                @pl.when(here.first_layer)
+                def _():
+                    get_middle(chunk, far(step)).start()
+
+        when(handled(get_table, chunk, far(step)), action)
+
+    def pass_on(chunk):
+        if get_table[chunk][3]:
+
+            @pl.when(here.first_layer)
+            def _():
+                for k in range(2):
+                    get_middle(chunk, 2 * (1 - here.home) + k).wait_recv()
+
+        get_across(chunk).start()
+
+    def gather(on_chunk):
+        last = len(get_table)
+        window = 2
+        for chunk in range(min(window, last)):
+            z_start(chunk)
+        one_step(0, 0)
+        for now in range(last + 4):
+            if now + 1 < last:
+                one_step(now + 1, 0)
+            if now < last:
+                for step in (1, 3, 2):
+                    one_step(now, step)
+            if now + window < last:
+                z_start(now + window)
+            if 0 <= now - 1 < last:
+                for step in range(4):
+                    two_steps(now - 1, step)
+            if 0 <= now - 2 < last:
+                for step in range(4):
+                    three_steps(now - 2, step)
+                if not get_table[now - 2][3]:
+                    pass_on(now - 2)
+            if 0 <= now - 3 < last and get_table[now - 3][3]:
+                pass_on(now - 3)
+            for chunk in (now - 3, now - 4):
+                if 0 <= chunk < last and get_table[chunk][3] == (chunk == now - 4):
+                    get_across(chunk).wait_recv()
+                    on_chunk(chunk)
+
+    def gathered():
+        for chunk in range(len(get_table)):
+            z_sent(chunk)
+            for step in range(4):
+
+                def action():
+                    get_first(chunk, step).wait_send()
+                    get_second(chunk, step).wait_send()
+
+                when(handled(get_table, chunk, far(step)), action)
+            if get_table[chunk][3]:
+
+                @pl.when(here.first_layer)
+                def _():
+                    for k in range(2):
+                        get_middle(chunk, 2 * here.home + k).wait_send()
+
+            get_across(chunk).wait_send()
+
+    def matrix(number, start, width):
+        ref = weight[number]
+        return ref[:, :, :, :, pl.ds(start, width)].reshape(features, width)
+
+    def in_rows(block, body):
+        lax.fori_loop(0, tokens // block, lambda i, c: (body(pl.ds(pl.multiple_of(i * block, block), block)), c)[1], 0)
+
+    def normed(rows, rows_in, normal, scale, gain):
+        centered = rows_in - jnp.mean(rows_in, axis=1, keepdims=True)
+        inv = lax.rsqrt(jnp.mean(centered * centered, axis=1, keepdims=True) + epsilon)
+        n = centered * inv
+        normal[rows] = n
+        scale[rows] = jnp.broadcast_to(inv, (n.shape[0], 128))
+        left[rows] = (n * gain).astype(low)
+
+    row_at = lax.broadcasted_iota(jnp.int32, (slots, 256), 0)
+    first_row = row_at == 0
+
+    def later(rows, places):
+        return jnp.where(row_at >= places, pltpu.roll(rows, places, 0), 0.0)
+
+    def sooner(rows, places):
+        return jnp.where(row_at < slots - places, pltpu.roll(rows, slots - places, 0), 0.0)
+
+    cuts = features // 256
+
+    def mixer_blocks(body, start=0, stop=None):
+        def step(i, carry):
+            m, cut = i // cuts, i % cuts
+            rows = pl.ds(pl.multiple_of(m * slots, slots), slots)
+            taken = pl.ds(pl.multiple_of(cut * 256, 256), 256)
+            body(m, rows, taken, cut)
+            return carry
+
+        lax.fori_loop(start, micro * cuts if stop is None else stop, step, 0)
+
+    def live_rows(m):
+        return (row_at.astype(f32) < jnp.concatenate([live[m, 0:1, :]] * 2, axis=1)).astype(f32)
+
+    def to_sibling(number, source, target):
+        return remote(source, target, send.at[number], recv.at[number], here.sibling())
+
+    def left_copy(k):
+        return to_sibling(k, lefts[k].at[0], lefts[k].at[1])
+
+    def right_sides(k):
+        return (
+            (projected, other_projected),
+            (after_low, other_after),
+            (expanded, other_expanded),
+            (active, other_active),
+        )[k]
+
+    def right_copy(k):
+        source, target = right_sides(k)
+        half = widths[1 + k] // 2
+        cut = pl.ds(pl.multiple_of((1 - here.core) * half, 128), half)
+        return to_sibling(4 + k, source.at[:, cut], target)
+
+    def small_copy():
+        return to_sibling(8, small_terms.at[1 - here.core], other_small)
+
+    give_out = remote(out_low, arrive, swap_sems.at[0], swap_sems.at[1], partner)
+    give_grad = remote(grad_low, arrive, swap_sems.at[0], swap_sems.at[1], partner)
+
+    def enter():
+        filt[...] = matrix(0, 0, 128).astype(f32).T
+        rows8[...] = matrix(0, 128, 128).astype(f32).T[:8]
+        in_rows(64, lambda rows: normed(rows, x_in[rows].astype(f32), norm_one, scale_one, rows8[3:4]))
+        lefts[0][0] = left[...].T
+        left_copy(0).start()
+
+    def mix(m, rows, taken, cut):
+        taps = [rows8[j : j + 1, taken] for j in range(3)]
+        alive = live_rows(m)
+        k = keys[rows, taken] * alive
+        keys[rows, taken] = k
+        v = values[rows, taken] * alive
+        kernel = filt[:, taken] + taps[0] * k + taps[1] * later(k, 1) + taps[2] * later(k, 2)
+        spec = left_dot(dft[...], parts(jnp.concatenate([v, kernel], axis=1)))
+        value_spec[m, :, taken] = spec[:, :256]
+        kernel_spec[m, :, taken] = spec[:, 256:]
+        v_re, v_im = spec[:slots, :256], spec[slots:, :256]
+        k_re, k_im = spec[:slots, 256:], spec[slots:, 256:]
+        both = k_im * v_im
+        re = k_re * v_re - jnp.where(first_row, 0.0, both)
+        im = jnp.where(first_row, both, k_re * v_im + k_im * v_re)
+        out = left_dot(idft[...], parts(jnp.concatenate([re, im], axis=0)))
+        convolved[rows, taken] = out
+        left[rows, taken] = (queries[rows, taken] * out).astype(low)
+
+    def mixer():
+        for k, target in enumerate((queries, keys, values)):
+            target[...] = left_dot(left[...], matrix(1, k * features, features))
+        mixer_blocks(mix)
+        lefts[1][0] = left[...].T
+        left_copy(1).start()
+
+    def mixer_out():
+        total[...] = x_in[...].astype(f32) + left_dot(left[...], matrix(2, 0, features))
+        in_rows(64, lambda rows: normed(rows, total[rows], norm_two, scale_two, rows8[4:5]))
+        lefts[2][0] = left[...].T
+        left_copy(2).start()
+
+    tile = 512
+
+    def tiles(start, width, body):
+        lax.fori_loop(0, width // tile, lambda i, c: (body(pl.multiple_of(start + i * tile, 128)), c)[1], 0)
+
+    def expand(start):
+        gate = left_dot(left[...], matrix(3, start, tile))
+        up = left_dot(left[...], matrix(3, pl.multiple_of(hidden + start, 128), tile))
+        expanded[:, pl.ds(start, tile)] = gate.astype(low)
+        expanded[:, pl.ds(pl.multiple_of(hidden + start, 128), tile)] = up.astype(low)
+        active[:, pl.ds(start, tile)] = (gate * jax.nn.sigmoid(gate) * up).astype(low)
+
+    def reduce_on(start, width):
+        total[...] += dot_back(active[:, pl.ds(start, width)], matrix(4, start, width))
+
+    def layer_done():
+        right_copy(3).start()
+        out_low[...] = total[...].astype(low)
+
+    ends = {array: max(k for k, entry in enumerate(get_table) if entry[0] == array) for array in range(5)}
+
+    def as_it_comes(chunk):
+        array, start, width, _ = get_table[chunk]
+
+        @pl.when(here.first_layer)
+        def _():
+            if array == 0:
+                x_in[...] = feed[...]
+                enter()
+            if array == 1 and ends[1] == chunk:
+                mixer()
+            if array == 2 and ends[2] == chunk:
+                mixer_out()
+            if array == 3:
+                tiles(start, width, expand)
+            if array == 4:
+                for half in (0, 1):
+                    reduce_on(half * (hidden // 2) + start, width)
+
+    def on_chunk(chunk):
+        if chunk == ends[0]:
+            fed()
+        as_it_comes(chunk)
+
+    gather(on_chunk)
+
+    @pl.when(here.first_layer)
+    def _():
+        layer_done()
+        give_out.start()
+        gathered()
+        give_grad.wait_recv()
+        e_in[...] = arrive[...]
+
+    @pl.when(here.second_layer)
+    def _():
+        gathered()
+        give_out.wait_recv()
+        x_in[...] = arrive[...]
+        e_in[...] = feed[...]
+        enter()
+        mixer()
+        mixer_out()
+
+        def both(start):
+            expand(start)
+            reduce_on(start, tile)
+
+        tiles(0, hidden, both)
+        layer_done()
+
+    lefts[3][0] = e_in[...].T
+    left_copy(3).start()
+    total[...] = jnp.zeros_like(total)
+
+    def expand_back(start):
+        again = pl.multiple_of(hidden + start, 128)
+        grad_act = left_dot(e_in[...], matrix(4, start, tile))
+        gate = expanded[:, pl.ds(start, tile)].astype(f32)
+        up = expanded[:, pl.ds(again, tile)].astype(f32)
+        sig = jax.nn.sigmoid(gate)
+        grad_gate = (grad_act * up * (sig * (1.0 + gate * (1.0 - sig)))).astype(low)
+        grad_up = (grad_act * (gate * sig)).astype(low)
+        expanded[:, pl.ds(start, tile)] = grad_gate
+        expanded[:, pl.ds(again, tile)] = grad_up
+        total[...] += dot_back(grad_gate, matrix(3, start, tile)) + dot_back(grad_up, matrix(3, again, tile))
+
+    tiles(0, hidden, expand_back)
+    right_copy(2).start()
+    for side in (here.x_side(), here.y_side()):
+        pl.semaphore_signal(ready, inc=1, device_id=side, device_id_type=MESH)
+
+    @pl.when(here.first_layer)
+    def _():
+        pl.semaphore_signal(ready, inc=1, device_id=here.middle(), device_id_type=MESH)
+
+    def norm_grad(rows, grad, normal, scale, gain, at):
+        n = normal[rows]
+        small_terms[1, at : at + 1] += jnp.sum(grad * n, axis=0, keepdims=True)
+        q = grad * gain
+        back = q - jnp.mean(q, axis=1, keepdims=True) - n * jnp.mean(q * n, axis=1, keepdims=True)
+        return scale[rows][:, :1] * back
+
+    def after_back():
+        small_terms[...] = jnp.zeros_like(small_terms)
+
+        def body(rows):
+            grad = e_in[rows].astype(f32) + norm_grad(rows, total[rows], norm_two, scale_two, rows8[4:5], 4)
+            after[rows] = grad
+            after_low[rows] = grad.astype(low)
+
+        in_rows(64, body)
+        right_copy(1).start()
+
+    def gated_back():
+        total[...] = dot_back(after_low[...], matrix(2, 0, features))
+
+    def mix_back(m, rows, taken, cut):
+        taps = [rows8[j : j + 1, taken] for j in range(3)]
+        alive = live_rows(m)
+        grad = total[rows, taken]
+        projected[rows, taken] = (grad * convolved[rows, taken]).astype(low)
+        spec = left_dot(dft[...], parts(grad * queries[rows, taken]))
+        g_re, g_im = spec[:slots], spec[slots:]
+        pairs = []
+        for other in (kernel_spec, value_spec):
+            o_re, o_im = other[m, :slots, taken], other[m, slots:, taken]
+            both = o_im * g_im
+            re = o_re * g_re + jnp.where(first_row, 0.0, both)
+            im = jnp.where(first_row, both, o_re * g_im - o_im * g_re)
+            pairs.append(jnp.concatenate([re, im], axis=0))
+        paired = left_dot(idft[...], parts(jnp.concatenate(pairs, axis=1)))
+        at_values = pl.ds(pl.multiple_of(2 * features + cut * 256, 256), 256)
+        projected[rows, at_values] = (paired[:, :256] * alive).astype(low)
+        grad_kernel = paired[:, 256:]
+        small_terms[0, :, taken] += grad_kernel
+        k = keys[rows, taken]
+        for j in range(3):
+            moved = later(k, j) if j else k
+            small_terms[1, j : j + 1, taken] += jnp.sum(grad_kernel * moved, axis=0, keepdims=True)
+        grad_keys = taps[0] * grad_kernel + taps[1] * sooner(grad_kernel, 1) + taps[2] * sooner(grad_kernel, 2)
+        at_keys = pl.ds(pl.multiple_of(features + cut * 256, 256), 256)
+        projected[rows, at_keys] = (grad_keys * alive).astype(low)
+
+    def mixed_back(start, stop):
+        mixer_blocks(mix_back, start, stop)
+        if stop == micro * cuts:
+            right_copy(0).start()
+
+    def input_back():
+        total[...] = dot_back(projected[...], matrix(1, 0, 3 * features))
+
+        def body(rows):
+            grad = after[rows] + norm_grad(rows, total[rows], norm_one, scale_one, rows8[3:4], 3)
+            grad_low[rows] = grad.astype(low)
+
+        in_rows(64, body)
+        small_copy().start()
+
+    half_way = micro * cuts // 2
+    pieces = [
+        after_back,
+        gated_back,
+        functools.partial(mixed_back, 0, half_way),
+        functools.partial(mixed_back, half_way, micro * cuts),
+        input_back,
+    ]
+
+    @pl.when(here.second_layer)
+    def _():
+        for piece in pieces:
+            piece()
+        give_grad.start()
+
+    offsets, place = [], 0
+    for array, _, width, _ in put_table:
+        offsets.append(place)
+        place += width if array else 0
+
+    def room(chunk):
+        return pl.ds(offsets[chunk], put_table[chunk][2])
+
+    def one_in(chunk, z):
+        if put_table[chunk][0] == 0:
+            return one_small.at[z]
+        return weight[3].at[z, 0, :, :, room(chunk)]
+
+    def two_in(chunk, z):
+        if put_table[chunk][0] == 0:
+            return two_small.at[z]
+        return weight[3].at[z, 1, 0, :, room(chunk)]
+
+    def mid_in(chunk, z, k):
+        return weight[3].at[z, 1, 1, k, :, room(chunk)]
+
+    def put_first(chunk, step):
+        z = far(step)
+        if step % 2:
+            source, side = mine[chunk].at[z, :, 1 - here.x], here.x_side()
+        else:
+            source, side = mine[chunk].at[z, 1 - here.y], here.y_side()
+        return remote(source, one_in(chunk, step), one_send.at[chunk, step], one_recv.at[chunk, step], side)
+
+    def put_second(chunk, step):
+        z = far(step)
+        if step % 2:
+            source, side = mine[chunk].at[z, 1 - here.y, here.x], here.y_side()
+        else:
+            source, side = mine[chunk].at[z, here.y, 1 - here.x], here.x_side()
+        return remote(source, two_in(chunk, step), two_send.at[chunk, step], two_recv.at[chunk, step], side)
+
+    def put_third(chunk, step, act):
+        z = far(step)
+        source = mine[chunk].at[z, here.y, here.x]
+        target = landed[put_table[chunk][0]].at[here.home, :, columns(put_table, chunk, here.core)]
+        receive = z_recv.at[chunk, here.home, here.core]
+        own = (here.z == z) & (here.core == here.layer)
+        if act == "start":
+
+            @pl.when(own)
+            def _():
+                pltpu.make_async_copy(source, target, receive).start()
+
+        @pl.when(jnp.logical_not(own))
+        def _():
+            away = remote(source, target, z_send.at[chunk, step], receive, (here.layer, here.chip(z=z)))
+            getattr(away, act)()
+
+    def add(target, other):
+        target[...] = (target[...].astype(f32) + other[...].astype(f32)).astype(target.dtype)
+
+    waits = [False] * 5
+
+    def terms(chunk):
+        array, start, width, shared = put_table[chunk]
+        if array == 0:
+            small_copy().wait_recv()
+            block = (small_terms[here.core] + other_small[...]).T
+        else:
+            if not waits[array]:
+                waits[array] = True
+                left_copy(array - 1).wait_recv()
+                right_copy(array - 1).wait_recv()
+            source, other = right_sides(array - 1)
+            own_at = pl.multiple_of(here.core * (widths[array] // 2) + start, 128)
+            block = left_dot(lefts[array - 1][0], source[:, pl.ds(own_at, width)])
+            block += left_dot(lefts[array - 1][1], other[:, pl.ds(start, width)])
+        block = block.astype(low)
+        rows = features // 16
+        for z in range(4):
+            for k in range(4):
+                at = (z * 4 + k) * rows
+                mine[chunk][z, k // 2, k % 2] = block[at : at + rows]
+        for step in range(4):
+            put_first(chunk, step).start()
+
+    def sum_one(chunk):
+        for step in range(4):
+            z = far(step)
+            put_first(chunk, step).wait_recv()
+            for k in range(2):
+                if step % 2:
+                    add(mine[chunk].at[z, k, here.x], one_in(chunk, step).at[k])
+                else:
+                    add(mine[chunk].at[z, here.y, k], one_in(chunk, step).at[k])
+            put_second(chunk, step).start()
+
+    def sum_two(chunk):
+        for step in range(4):
+            put_second(chunk, step).wait_recv()
+            add(mine[chunk].at[far(step), here.y, here.x], two_in(chunk, step))
+            put_third(chunk, step, "start")
+
+    pl.when(here.first_layer)(lambda: pl.semaphore_wait(ready, 3))
+    pl.when(here.second_layer)(lambda: pl.semaphore_wait(ready, 2))
+
+    apart = here.core != here.layer
+    over = (1 - here.core, here.partner)
+
+    def swap(source, target, number, act):
+        sems = swap_sems.at[number], swap_sems.at[number + 1]
+
+        @pl.when(apart)
+        def _():
+            getattr(remote(source, target, *sems, over), act)()
+
+        @pl.when(jnp.logical_not(apart))
+        def _():
+            getattr(pltpu.make_async_copy(source, target, sems[1]), act)()
+
+    last = len(put_table)
+    needs = {array: min(k for k, entry in enumerate(put_table) if entry[0] == array) for array in range(5)}
+    due = [max(0, needs[1] - 5 + k) for k in range(4)] + [needs[0] - 2]
+    terms(0)
+    swap(out_low, kept_out, 2, "start")
+    for now in range(last + 1):
+        for piece, at in zip(pieces, due):
+            if at == now:
+                pl.when(here.first_layer)(piece)
+        if now + 1 < last:
+            terms(now + 1)
+        if now < last:
+            sum_one(now)
+        if 1 <= now:
+            sum_two(now - 1)
+        if now == needs[0]:
+            swap(grad_low, kept_grad, 4, "start")
+
+    for chunk in range(last):
+        for half in (0, 1):
+            for slot in (0, 1):
+                target = landed[put_table[chunk][0]].at[slot, :, columns(put_table, chunk, half)]
+                arrived(target, z_recv.at[chunk, slot, half])
+        for step in range(4):
+            put_first(chunk, step).wait_send()
+            put_second(chunk, step).wait_send()
+            put_third(chunk, step, "wait_send")
+
+    @pl.when(own_feed)
+    def _():
+        remote(hidden_in, feed, feed_sems.at[1], feed_sems.at[0], partner).wait_send()
+        remote(live_own, live, feed_sems.at[3], feed_sems.at[2], partner).wait_send()
+
+    for k in range(4):
+        left_copy(k).wait_send()
+        right_copy(k).wait_send()
+    small_copy().wait_send()
+    give_out.wait_send()
+    swap(out_low, kept_out, 2, "wait")
+    swap(grad_low, kept_grad, 4, "wait")
+
+
+def finish_kernel(*refs):
+    landed, (out, grad) = refs[:5], refs[5:7]
+    s_filters, s_taps, s_one, s_two = refs[7:11]
+    sums, (to_out, to_grad), sems = refs[11:15], refs[15:17], refs[17]
+    copies = [pltpu.make_async_copy(out, to_out, sems.at[0]), pltpu.make_async_copy(grad, to_grad, sems.at[1])]
+    for copy in copies:
+        copy.start()
+    small = landed[0][0].astype(jnp.float32) + landed[0][1].astype(jnp.float32)
+    s_filters[...] = small[:, :128]
+    own = small.shape[0]
+    rows = jnp.pad(small[:, 128:], ((0, 128 - own), (0, 0))).T
+    s_taps[...] = rows[0:3, :own]
+    s_one[...] = rows[3:4, :own]
+    s_two[...] = rows[4:5, :own]
+    for number, result in enumerate(sums):
+        result[...] = landed[1 + number][0].astype(jnp.float32) + landed[1 + number][1].astype(jnp.float32)
+    for copy in copies:
+        copy.wait()
+
+
+def fast_device(
+    hidden_in, out_grad, lengths, gain_mixer, w_input, w_taps, filters, w_output, gain_mlp, w_gate_up, w_down
+):
+    micro, _, slots, features = hidden_in.shape
+    tokens, rows = micro * slots, gain_mixer.shape[1]
+    shards = (w_input[0], w_output[0], w_gate_up[0], w_down[0].T)
+    widths = [256] + [shard.shape[1] for shard in shards]
+    hidden = widths[4]
+    get_table, put_table = chunks_of(GET_PIECES), chunks_of(PUT_PIECES)
+    dft, idft = (jnp.asarray(table) for table in packed_tables(slots))
+    low, f32 = jnp.bfloat16, jnp.float32
+    anywhere = pl.BlockSpec(memory_space=pl.ANY)
+    inside = pl.BlockSpec(memory_space=pltpu.VMEM)
+    dma, vmem = pltpu.SemaphoreType.DMA, pltpu.VMEM
+    act, act_low = (tokens, features), vmem((tokens, features), low)
+    kinds = [jax.ShapeDtypeStruct((2, rows, width), low) for width in widths]
+    kinds += [jax.ShapeDtypeStruct((tokens, features), low)] * 2
+    room = [vmem((rows, 256), low), vmem((128, 128), f32)] + [vmem((micro, 8, 128), f32)] * 2
+    room += [vmem((4, 2, 2, rows, width), low) for width in widths]
+    room += [act_low] * 6
+    room += [vmem((slots, features), f32), vmem((8, features), f32), vmem(act, f32), vmem(act, f32)]
+    room += [vmem((tokens, 128), f32)] * 2
+    room += [act_low] + [vmem(act, f32)] * 4 + [vmem((micro, 2 * slots, features), f32)] * 2
+    room += [vmem(act, f32)] * 2 + [vmem((tokens, 2 * hidden), low), vmem((tokens, hidden), low)]
+    room += [vmem((tokens, 3 * features), low), act_low, vmem((2, slots, features), f32)]
+    room += [vmem((2, features, tokens), low)] * 4
+    room += [vmem((slots, features), f32)] + [vmem((tokens, width // 2), low) for width in widths[1:]]
+    room += [vmem((4, 2, 2, rows, entry[2]), low) for entry in put_table]
+    room += [vmem((4, 2, rows, 128), low), vmem((4, rows, 128), low)]
+    got, put = len(get_table), len(put_table)
+    room += [dma((got, 2, 2))] + [dma((got, 4))] * 5 + [dma((got, 2))] * 2 + [dma((got,))] * 2 + [dma((4,))]
+    room += [dma((6,)), dma((9,)), dma((9,))]
+    room += [dma((put, 4))] * 5 + [dma((put, 2, 2))] + [dma((put,))] * 2 + [pltpu.SemaphoreType.REGULAR]
+    results = pl.pallas_call(
+        functools.partial(layer_kernel, get_table, put_table, widths),
+        out_shape=kinds,
+        in_specs=[inside] * 4 + [pl.BlockSpec(memory_space=pltpu.SMEM)] + [inside] * 2 + [anywhere] * 6,
+        out_specs=[anywhere] * 7,
+        scratch_shapes=room,
+        compiler_params=pltpu.CompilerParams(
+            collective_id=0, has_side_effects=True, vmem_limit_bytes=62 * 1024 * 1024
+        ),
+    )(
+        filters[0].T,
+        w_taps[0],
+        gain_mixer,
+        gain_mlp,
+        lengths,
+        dft,
+        idft,
+        *shards,
+        hidden_in.reshape(tokens, features),
+        out_grad.reshape(tokens, features),
+    )
+    kinds = [(rows, 128), (3, rows), (1, rows), (1, rows)] + [(rows, width) for width in widths[1:]]
+    kinds = [jax.ShapeDtypeStruct(kind, f32) for kind in kinds] + kinds_of(results[5:])
+    s_filters, s_taps, s_one, s_two, s_in, s_out, s_gu, s_dt, layer_out, input_grad = pl.pallas_call(
+        finish_kernel,
+        out_shape=kinds,
+        in_specs=[inside] * 5 + [anywhere] * 2,
+        out_specs=[inside] * 8 + [anywhere] * 2,
+        scratch_shapes=[dma((2,))],
+        compiler_params=pltpu.CompilerParams(vmem_limit_bytes=32 * 1024 * 1024),
+    )(*results)
+    shape = (1, micro, 1, slots, features)
+    return (
+        layer_out.reshape(shape),
+        input_grad.reshape(shape),
+        s_one,
+        s_in[None],
+        s_taps[None],
+        s_filters.T[None],
+        s_out[None],
+        s_two,
+        s_gu[None],
+        s_dt.T[None],
+    )
+
+
+def kinds_of(arrays):
+    return [jax.ShapeDtypeStruct(array.shape, array.dtype) for array in arrays]
+
+
 def solution(mesh):
     placed = (
         P(None, "dp", None, None),
@@ -415,7 +1293,7 @@
         P("section", None, "dp"),
     )
     return jax.shard_map(
-        on_device,
+        fast_device if mesh.shape["dp"] == 16 and mesh.shape["section"] == 2 else on_device,
         mesh=mesh,
         in_specs=placed,
         out_specs=(

time: 1100 us -> 262 us (0.24)
  waiting for transfers between devices: 361 us -> 0 us
  Pallas kernels: 0 us -> 247 us
  other arithmetic: 216 us -> 0 us
  local copies, waits for them, and re-layouts: 196 us -> 8.9 us
  matrix products: 120 us -> 0 us
  blocking collectives: 114 us -> 0 us
  starting transfers between devices: 64.4 us -> 0 us
  between operations: 18.7 us -> 0.67 us
    pallas_call x0 -> x2, Pallas kernels: none -> 247 us  [the longest x1 245 us: fast_device(): pl.pallas_call(functools.partial(layer_kernel, get_table, put_table, widt...]
    all_gather x4 -> x0, waiting for transfers between devices: 192 us -> none  [the longest x1 118 us: on_device(): lax.all_gather(w_gate_up[0], 'dp', axis=0, tiled=True)]
    unnamed x7 -> x0, other arithmetic: 171 us -> none
    all_to_all x8 -> x0, waiting for transfers between devices: 165 us -> none  [the longest x1 138 us: on_device(): lax.all_to_all(mlp_totals[1][None].astype(jnp.bfloat16), 'dp', split_axis...]
    unnamed x311 -> x16, local copies, waits for them, and re-layouts: 131 us -> 8.9 us
    dot_general x48 -> x0, matrix products: 120 us -> none  [the longest x12 45 us: dot_rows(): lax.dot_general(left_side, right_side, (((0,), (0,)), ((), ())), preferre...]
    all_gather x2 -> x0, blocking collectives: 78.2 us -> none  [the longest x1 40.1 us: on_device(): lax.all_gather(filters[0], 'dp', axis=1, tiled=True)]
    all_to_all x8 -> x0, starting transfers between devices: 56.6 us -> none  [the longest x1 8.14 us: on_device(): lax.all_to_all(mixer_totals[2].T[None].astype(jnp.bfloat16), 'dp', split_...]
  transfers between devices with their start and end apart: 16 -> 0, of which waited for: 9 -> 0; matrix products, arithmetic and copies ran while one was open for 38% -> 0% of each run, Pallas kernels for 0% -> 0%
where the time goes in v1:
time: 262 us; the launch traced here: 257 us
  Pallas kernels  247 us (94%)
  local copies, waits for them, and re-layouts  8.9 us (3%)
    pallas_call x1, Pallas kernels, fast_device(): pl.pallas_call(functools.partial(layer_kernel, get_table, put_table, widt...  245 us
    unnamed x16, local copies, waits for them, and re-layouts  8.9 us

profile of v1, /device:TPU:28, one launch (start us, length us, event | category | flops | bytes accessed | tf_op | source)
XLA Modules:
  0.0 257.0 jit_solution(14468281110969966714)
XLA Ops:
  0.6 1.3 copy.23.refs_4_
  1.9 245.1 %shard_map.204 = (bf16[2,48,256]{2,1,0:T(8,128)(2,1)}, bf16[2,48,2304]{2,1,0:T(8,128)(2,1)}, bf16[2,48,768]{2,1,0:T(8,128)(2,1)}, bf16[2,48,6144]{2,1,0:T(8,128)...) custom-call(bf16[48,128]{1,0:T(8,128)(2,1)} %bitcast.35, ...), custom_call_target="tpu_custom_call" | custom-call | tf_op jit(solution)/shard_map/pallas_call | solution.py:1231
  247.0 0.0 copy-start
  247.0 1.3 copy-done
  248.3 0.0 copy-start.1
  248.3 1.1 copy-done.1
  249.4 0.0 copy-start.2
  249.4 1.0 copy-done.2
  250.4 0.0 copy-start.3
  250.4 1.0 copy-done.3
  251.4 0.0 copy-start.4
  251.4 1.0 copy-done.4
  252.4 0.0 copy-start.5
  252.4 0.9 copy-done.5
  253.3 0.0 copy-start.6
  253.3 0.8 copy-done.6
  254.1 2.3 shard_map.205
  256.4 0.6 copy.26
Async XLA Ops:
  247.0 1.3 copy-start
  248.3 1.1 copy-start.1
  249.4 1.0 copy-start.2
  250.4 1.0 copy-start.3
  251.4 1.0 copy-start.4
  252.4 0.9 copy-start.5
  253.3 0.8 copy-start.6

commit v2 on v1

--- a/solution.py
+++ b/solution.py
@@ -38,6 +38,10 @@
     (1, 384, False),
     (0, 128, False),
 )
+GET_LAGS = (5, 9, 1, 2, 3)
+ROWS_UNROLL = 2
+MIX_UNROLL = 3
+TILE_UNROLL = 2
 
 
 def passed_along(value, axis, steps):
@@ -498,6 +502,10 @@
     )
 
 
+def sigmoid(value):
+    return 0.5 * jnp.tanh(0.5 * value) + 0.5
+
+
 def parts(signal):
     high = signal.astype(jnp.bfloat16)
     rest = (signal - high.astype(jnp.float32)).astype(jnp.bfloat16)
@@ -535,7 +543,7 @@
     weight = take(5)
     feed, arrive, x_in, e_in, out_low, grad_low = take(6)
     filt, rows8, norm_one, norm_two, scale_one, scale_two = take(6)
-    left, queries, keys, values, convolved, value_spec, kernel_spec = take(7)
+    entered, gated, again, queries, keys, values, convolved, value_spec, kernel_spec = take(9)
     total, after, expanded, active, projected, after_low, small_terms = take(7)
     lefts = take(4)
     other_small, other_projected, other_after, other_expanded, other_active = take(5)
@@ -543,7 +551,7 @@
     one_small, two_small = take(2)
     get_z_send, get_z_recv, get_one_send, get_one_recv, get_two_send, get_two_recv = take(6)
     get_mid_send, get_mid_recv, get_side_send, get_side_recv, feed_sems = take(5)
-    swap_sems, send, recv = take(3)
+    swap_sems, give_send, give_recv, send, recv = take(5)
     one_send, one_recv, two_send, two_recv, z_send, z_recv, mid_send, mid_recv, ready = take(9)
 
     here = Place()
@@ -562,7 +570,7 @@
     own_small[:, :128] = filters_in[...]
     own_small[:, 128:] = rows_in[...].T[:own].astype(low)
     for m in range(micro):
-        live_own[m] = jnp.full(live_own.shape[1:], lengths_in[m, 0], jnp.int32).astype(f32)
+        live_own[m] = jnp.full(live_own.shape[1:], lengths_in[0, m], jnp.int32).astype(f32)
     here.greet()
 
     own_feed = here.core == here.layer
@@ -596,19 +604,28 @@
         else:
             pl.when(condition)(action)
 
-    def z_all(chunk, visit):
+    def z_all(chunk, visit, near):
         array, _, _, shared = get_table[chunk]
         for number, plane in enumerate((1 - here.core, 2 + here.core)):
-            wanted = (here.core == 1) | (here.home == number) if shared else here.z >= 0
+            wanted = (plane == here.z) if near else (plane != here.z)
+            if shared:
+                wanted = wanted & ((here.core == 1) | (here.home == number))
             for half in (0, 1):
-                own = (plane == here.z) & (here.core == half)
                 cut = columns(get_table, chunk, half)
                 source, target = shards[array].at[:, cut], weight[array].at[here.z, here.y, here.x, :, cut]
                 sems = get_z_send.at[chunk, number, half], get_z_recv.at[chunk, here.z]
-                visit(wanted, own, source, target, sems, (half, here.chip(z=plane)))
-
-    def z_start(chunk):
+                visit(wanted, here.core == half, source, target, sems, (half, here.chip(z=plane)))
+
+    def z_start(chunk, near):
         def visit(wanted, own, source, target, sems, device):
+            if not near:
+
+                @pl.when(wanted)
+                def _():
+                    remote(source, target, *sems, device).start()
+
+                return
+
             @pl.when(wanted & own)
             def _():
                 pltpu.make_async_copy(source, target, sems[1]).start()
@@ -617,15 +634,17 @@
             def _():
                 remote(source, target, *sems, device).start()
 
-        z_all(chunk, visit)
+        z_all(chunk, visit, near)
 
     def z_sent(chunk):
-        def visit(wanted, own, source, target, sems, device):
-            @pl.when(wanted & jnp.logical_not(own))
-            def _():
-                remote(source, target, *sems, device).wait_send()
-
-        z_all(chunk, visit)
+        for near in (False, True):
+
+            def visit(wanted, own, source, target, sems, device):
+                @pl.when(wanted & jnp.logical_not(own) if near else wanted)
+                def _():
+                    remote(source, target, *sems, device).wait_send()
+
+            z_all(chunk, visit, near)
 
     def far(step):
         return (here.z + step) % 4
@@ -635,12 +654,12 @@
 
     def get_first(chunk, step):
         block = weight[get_table[chunk][0]].at[far(step), here.y, here.x, :, columns(get_table, chunk, here.core)]
-        side = here.y_side() if step % 2 else here.x_side()
+        side = here.y_side() if (step + chunk) % 2 else here.x_side()
         return remote(block, block, get_one_send.at[chunk, step], get_one_recv.at[chunk, step], side)
 
     def get_second(chunk, step):
         ref, cut = weight[get_table[chunk][0]], columns(get_table, chunk, here.core)
-        if step % 2:
+        if (step + chunk) % 2:
             pair, side = ref.at[far(step), :, here.x, :, cut], here.x_side()
         else:
             pair, side = ref.at[far(step), here.y, :, :, cut], here.y_side()
@@ -693,30 +712,42 @@
 
     def gather(on_chunk):
         last = len(get_table)
-        window = 2
-        for chunk in range(min(window, last)):
-            z_start(chunk)
-        one_step(0, 0)
-        for now in range(last + 4):
-            if now + 1 < last:
-                one_step(now + 1, 0)
+        ahead, own_ahead, two_lag, three_lag, done_lag = GET_LAGS
+        for chunk in range(last):
+            z_start(chunk, True)
+
+        def z_first():
+            for chunk in range(min(ahead, last)):
+                z_start(chunk, False)
+
+        pl.when(here.core == 0)(z_first)
+        for chunk in range(min(own_ahead, last)):
+            one_step(chunk, 0)
+        for chunk in range(min(own_ahead, last) - 1):
+            two_steps(chunk, 0)
+        pl.when(here.core == 1)(z_first)
+        for now in range(last + done_lag + 1):
+            if now + own_ahead < last:
+                one_step(now + own_ahead, 0)
+            if 0 <= now + own_ahead - 1 < last:
+                two_steps(now + own_ahead - 1, 0)
             if now < last:
                 for step in (1, 3, 2):
                     one_step(now, step)
-            if now + window < last:
-                z_start(now + window)
-            if 0 <= now - 1 < last:
+            if now + ahead < last:
+                z_start(now + ahead, False)
+            if 0 <= now - two_lag < last:
+                for step in (1, 3, 2):
+                    two_steps(now - two_lag, step)
+            if 0 <= now - three_lag < last:
                 for step in range(4):
-                    two_steps(now - 1, step)
-            if 0 <= now - 2 < last:
-                for step in range(4):
-                    three_steps(now - 2, step)
-                if not get_table[now - 2][3]:
-                    pass_on(now - 2)
-            if 0 <= now - 3 < last and get_table[now - 3][3]:
-                pass_on(now - 3)
-            for chunk in (now - 3, now - 4):
-                if 0 <= chunk < last and get_table[chunk][3] == (chunk == now - 4):
+                    three_steps(now - three_lag, step)
+                if not get_table[now - three_lag][3]:
+                    pass_on(now - three_lag)
+            if 0 <= now - three_lag - 1 < last and get_table[now - three_lag - 1][3]:
+                pass_on(now - three_lag - 1)
+            for chunk in (now - done_lag, now - done_lag - 1):
+                if 0 <= chunk < last and get_table[chunk][3] == (chunk == now - done_lag - 1):
                     get_across(chunk).wait_recv()
                     on_chunk(chunk)
 
@@ -743,16 +774,25 @@
         ref = weight[number]
         return ref[:, :, :, :, pl.ds(start, width)].reshape(features, width)
 
-    def in_rows(block, body):
-        lax.fori_loop(0, tokens // block, lambda i, c: (body(pl.ds(pl.multiple_of(i * block, block), block)), c)[1], 0)
-
-    def normed(rows, rows_in, normal, scale, gain):
+    def in_rows(body, start=0, count=tokens):
+        block = 64
+
+        def step(i, carry):
+            body(pl.ds(pl.multiple_of(start + i * block, block), block))
+            return carry
+
+        lax.fori_loop(0, count // block, step, 0, unroll=ROWS_UNROLL)
+
+    def sequence(m):
+        return pl.ds(pl.multiple_of(m * slots, slots), slots)
+
+    def normed(rows, rows_in, normal, scale, gain, target):
         centered = rows_in - jnp.mean(rows_in, axis=1, keepdims=True)
         inv = lax.rsqrt(jnp.mean(centered * centered, axis=1, keepdims=True) + epsilon)
         n = centered * inv
         normal[rows] = n
         scale[rows] = jnp.broadcast_to(inv, (n.shape[0], 128))
-        left[rows] = (n * gain).astype(low)
+        target[rows] = (n * gain).astype(low)
 
     row_at = lax.broadcasted_iota(jnp.int32, (slots, 256), 0)
     first_row = row_at == 0
@@ -765,15 +805,12 @@
 
     cuts = features // 256
 
-    def mixer_blocks(body, start=0, stop=None):
-        def step(i, carry):
-            m, cut = i // cuts, i % cuts
-            rows = pl.ds(pl.multiple_of(m * slots, slots), slots)
-            taken = pl.ds(pl.multiple_of(cut * 256, 256), 256)
-            body(m, rows, taken, cut)
+    def mixer_blocks(m, body):
+        def step(cut, carry):
+            body(m, sequence(m), pl.ds(pl.multiple_of(cut * 256, 256), 256), cut)
             return carry
 
-        lax.fori_loop(start, micro * cuts if stop is None else stop, step, 0)
+        lax.fori_loop(0, cuts, step, 0, unroll=MIX_UNROLL)
 
     def live_rows(m):
         return (row_at.astype(f32) < jnp.concatenate([live[m, 0:1, :]] * 2, axis=1)).astype(f32)
@@ -801,15 +838,28 @@
     def small_copy():
         return to_sibling(8, small_terms.at[1 - here.core], other_small)
 
-    give_out = remote(out_low, arrive, swap_sems.at[0], swap_sems.at[1], partner)
-    give_grad = remote(grad_low, arrive, swap_sems.at[0], swap_sems.at[1], partner)
-
-    def enter():
+    def give(source, m):
+        rows = pl.ds(m * slots, slots)
+        return remote(source.at[rows], arrive.at[rows], give_send.at[m], give_recv.at[m], partner)
+
+    def received(target, m):
+        rows = sequence(m)
+        arrived(arrive.at[rows], give_recv.at[m])
+        target[rows] = arrive[rows]
+
+    def turned(k):
+        lefts[k][0] = (entered, gated, again, e_in)[k][...].T
+        left_copy(k).start()
+
+    def small_weights():
         filt[...] = matrix(0, 0, 128).astype(f32).T
         rows8[...] = matrix(0, 128, 128).astype(f32).T[:8]
-        in_rows(64, lambda rows: normed(rows, x_in[rows].astype(f32), norm_one, scale_one, rows8[3:4]))
-        lefts[0][0] = left[...].T
-        left_copy(0).start()
+
+    def enter(m):
+        def body(rows):
+            normed(rows, x_in[rows].astype(f32), norm_one, scale_one, rows8[3:4], entered)
+
+        in_rows(body, m * slots, slots)
 
     def mix(m, rows, taken, cut):
         taps = [rows8[j : j + 1, taken] for j in range(3)]
@@ -828,32 +878,46 @@
         im = jnp.where(first_row, both, k_re * v_im + k_im * v_re)
         out = left_dot(idft[...], parts(jnp.concatenate([re, im], axis=0)))
         convolved[rows, taken] = out
-        left[rows, taken] = (queries[rows, taken] * out).astype(low)
-
-    def mixer():
+        gated[rows, taken] = (queries[rows, taken] * out).astype(low)
+
+    def mixer(m):
+        rows = sequence(m)
         for k, target in enumerate((queries, keys, values)):
-            target[...] = left_dot(left[...], matrix(1, k * features, features))
-        mixer_blocks(mix)
-        lefts[1][0] = left[...].T
-        left_copy(1).start()
-
-    def mixer_out():
-        total[...] = x_in[...].astype(f32) + left_dot(left[...], matrix(2, 0, features))
-        in_rows(64, lambda rows: normed(rows, total[rows], norm_two, scale_two, rows8[4:5]))
-        lefts[2][0] = left[...].T
-        left_copy(2).start()
+            target[rows] = left_dot(entered[rows], matrix(1, k * features, features))
+        mixer_blocks(m, mix)
+
+    def mixer_out(m):
+        rows = sequence(m)
+        total[rows] = x_in[rows].astype(f32) + left_dot(gated[rows], matrix(2, 0, features))
+
+        def body(rows):
+            normed(rows, total[rows], norm_two, scale_two, rows8[4:5], again)
+
+        in_rows(body, m * slots, slots)
+
+    def each_sequence(*bodies):
+        def step(m, carry):
+            for body in bodies:
+                body(m)
+            return carry
+
+        lax.fori_loop(0, micro, step, 0)
 
     tile = 512
 
     def tiles(start, width, body):
-        lax.fori_loop(0, width // tile, lambda i, c: (body(pl.multiple_of(start + i * tile, 128)), c)[1], 0)
+        def step(i, carry):
+            body(pl.multiple_of(start + i * tile, 128))
+            return carry
+
+        lax.fori_loop(0, width // tile, step, 0, unroll=TILE_UNROLL)
 
     def expand(start):
-        gate = left_dot(left[...], matrix(3, start, tile))
-        up = left_dot(left[...], matrix(3, pl.multiple_of(hidden + start, 128), tile))
+        gate = left_dot(again[...], matrix(3, start, tile))
+        up = left_dot(again[...], matrix(3, pl.multiple_of(hidden + start, 128), tile))
         expanded[:, pl.ds(start, tile)] = gate.astype(low)
         expanded[:, pl.ds(pl.multiple_of(hidden + start, 128), tile)] = up.astype(low)
-        active[:, pl.ds(start, tile)] = (gate * jax.nn.sigmoid(gate) * up).astype(low)
+        active[:, pl.ds(start, tile)] = (gate * sigmoid(gate) * up).astype(low)
 
     def reduce_on(start, width):
         total[...] += dot_back(active[:, pl.ds(start, width)], matrix(4, start, width))
@@ -871,11 +935,15 @@
         def _():
             if array == 0:
                 x_in[...] = feed[...]
-                enter()
+                small_weights()
+                each_sequence(enter)
+                turned(0)
             if array == 1 and ends[1] == chunk:
-                mixer()
+                each_sequence(mixer)
+                turned(1)
             if array == 2 and ends[2] == chunk:
-                mixer_out()
+                each_sequence(mixer_out)
+                turned(2)
             if array == 3:
                 tiles(start, width, expand)
             if array == 4:
@@ -892,20 +960,20 @@
     @pl.when(here.first_layer)
     def _():
         layer_done()
-        give_out.start()
+        for m in range(micro):
+            give(out_low, m).start()
+            give(out_low, m).wait_send()
         gathered()
-        give_grad.wait_recv()
-        e_in[...] = arrive[...]
+        for m in range(micro):
+            received(e_in, m)
+        turned(3)
 
     @pl.when(here.second_layer)
     def _():
+        small_weights()
+        e_in[...] = feed[...]
         gathered()
-        give_out.wait_recv()
-        x_in[...] = arrive[...]
-        e_in[...] = feed[...]
-        enter()
-        mixer()
-        mixer_out()
+        each_sequence(functools.partial(received, x_in), enter, mixer, mixer_out)
 
         def both(start):
             expand(start)
@@ -914,8 +982,6 @@
         tiles(0, hidden, both)
         layer_done()
 
-    lefts[3][0] = e_in[...].T
-    left_copy(3).start()
     total[...] = jnp.zeros_like(total)
 
     def expand_back(start):
@@ -923,7 +989,7 @@
         grad_act = left_dot(e_in[...], matrix(4, start, tile))
         gate = expanded[:, pl.ds(start, tile)].astype(f32)
         up = expanded[:, pl.ds(again, tile)].astype(f32)
-        sig = jax.nn.sigmoid(gate)
+        sig = sigmoid(gate)
         grad_gate = (grad_act * up * (sig * (1.0 + gate * (1.0 - sig)))).astype(low)
         grad_up = (grad_act * (gate * sig)).astype(low)
         expanded[:, pl.ds(start, tile)] = grad_gate
@@ -954,7 +1020,7 @@
             after[rows] = grad
             after_low[rows] = grad.astype(low)
 
-        in_rows(64, body)
+        in_rows(body)
         right_copy(1).start()
 
     def gated_back():
@@ -987,35 +1053,42 @@
         at_keys = pl.ds(pl.multiple_of(features + cut * 256, 256), 256)
         projected[rows, at_keys] = (grad_keys * alive).astype(low)
 
-    def mixed_back(start, stop):
-        mixer_blocks(mix_back, start, stop)
-        if stop == micro * cuts:
-            right_copy(0).start()
-
-    def input_back():
-        total[...] = dot_back(projected[...], matrix(1, 0, 3 * features))
+    def mixed_back(m):
+        mixer_blocks(m, mix_back)
+
+    def input_back(m):
+        rows = sequence(m)
+        total[rows] = dot_back(projected[rows], matrix(1, 0, 3 * features))
 
         def body(rows):
             grad = after[rows] + norm_grad(rows, total[rows], norm_one, scale_one, rows8[3:4], 3)
             grad_low[rows] = grad.astype(low)
 
-        in_rows(64, body)
+        in_rows(body, m * slots, slots)
+
+    pieces = [after_back, gated_back]
+    for m in range(micro):
+        pieces += [functools.partial(mixed_back, m), functools.partial(input_back, m)]
+
+    def last_copies():
+        right_copy(0).start()
         small_copy().start()
 
-    half_way = micro * cuts // 2
-    pieces = [
-        after_back,
-        gated_back,
-        functools.partial(mixed_back, 0, half_way),
-        functools.partial(mixed_back, half_way, micro * cuts),
-        input_back,
-    ]
+    pieces += [last_copies]
 
     @pl.when(here.second_layer)
     def _():
-        for piece in pieces:
-            piece()
-        give_grad.start()
+        after_back()
+        gated_back()
+        for m in range(micro):
+            mixed_back(m)
+            input_back(m)
+            if m:
+                give(grad_low, m - 1).wait_send()
+            give(grad_low, m).start()
+        last_copies()
+        for k in (3, 2, 1, 0):
+            turned(k)
 
     offsets, place = [], 0
     for array, _, width, _ in put_table:
@@ -1135,9 +1208,9 @@
 
     last = len(put_table)
     needs = {array: min(k for k, entry in enumerate(put_table) if entry[0] == array) for array in range(5)}
-    due = [max(0, needs[1] - 5 + k) for k in range(4)] + [needs[0] - 2]
+    due = [max(0, needs[1] - len(pieces) + k) for k in range(len(pieces))]
     terms(0)
-    swap(out_low, kept_out, 2, "start")
+    swap(out_low, kept_out, 0, "start")
     for now in range(last + 1):
         for piece, at in zip(pieces, due):
             if at == now:
@@ -1149,7 +1222,7 @@
         if 1 <= now:
             sum_two(now - 1)
         if now == needs[0]:
-            swap(grad_low, kept_grad, 4, "start")
+            swap(grad_low, kept_grad, 2, "start")
 
     for chunk in range(last):
         for half in (0, 1):
@@ -1170,29 +1243,27 @@
         left_copy(k).wait_send()
         right_copy(k).wait_send()
     small_copy().wait_send()
-    give_out.wait_send()
-    swap(out_low, kept_out, 2, "wait")
-    swap(grad_low, kept_grad, 4, "wait")
+    pl.when(here.second_layer)(lambda: give(grad_low, micro - 1).wait_send())
+    swap(out_low, kept_out, 0, "wait")
+    swap(grad_low, kept_grad, 2, "wait")
 
 
 def finish_kernel(*refs):
     landed, (out, grad) = refs[:5], refs[5:7]
     s_filters, s_taps, s_one, s_two = refs[7:11]
-    sums, (to_out, to_grad), sems = refs[11:15], refs[15:17], refs[17]
-    copies = [pltpu.make_async_copy(out, to_out, sems.at[0]), pltpu.make_async_copy(grad, to_grad, sems.at[1])]
-    for copy in copies:
-        copy.start()
+    sums, (to_out, to_grad) = refs[11:15], refs[15:17]
+    to_out[...] = out[...]
+    to_grad[...] = grad[...]
     small = landed[0][0].astype(jnp.float32) + landed[0][1].astype(jnp.float32)
     s_filters[...] = small[:, :128]
     own = small.shape[0]
     rows = jnp.pad(small[:, 128:], ((0, 128 - own), (0, 0))).T
-    s_taps[...] = rows[0:3, :own]
+    for j in range(3):
+        s_taps[j] = rows[j : j + 1, :own]
     s_one[...] = rows[3:4, :own]
     s_two[...] = rows[4:5, :own]
     for number, result in enumerate(sums):
         result[...] = landed[1 + number][0].astype(jnp.float32) + landed[1 + number][1].astype(jnp.float32)
-    for copy in copies:
-        copy.wait()
 
 
 def fast_device(
@@ -1217,7 +1288,7 @@
     room += [act_low] * 6
     room += [vmem((slots, features), f32), vmem((8, features), f32), vmem(act, f32), vmem(act, f32)]
     room += [vmem((tokens, 128), f32)] * 2
-    room += [act_low] + [vmem(act, f32)] * 4 + [vmem((micro, 2 * slots, features), f32)] * 2
+    room += [act_low] * 3 + [vmem(act, f32)] * 4 + [vmem((micro, 2 * slots, features), f32)] * 2
     room += [vmem(act, f32)] * 2 + [vmem((tokens, 2 * hidden), low), vmem((tokens, hidden), low)]
     room += [vmem((tokens, 3 * features), low), act_low, vmem((2, slots, features), f32)]
     room += [vmem((2, features, tokens), low)] * 4
@@ -1226,7 +1297,7 @@
     room += [vmem((4, 2, rows, 128), low), vmem((4, rows, 128), low)]
     got, put = len(get_table), len(put_table)
     room += [dma((got, 2, 2))] + [dma((got, 4))] * 5 + [dma((got, 2))] * 2 + [dma((got,))] * 2 + [dma((4,))]
-    room += [dma((6,)), dma((9,)), dma((9,))]
+    room += [dma((4,)), dma((micro,)), dma((micro,)), dma((9,)), dma((9,))]
     room += [dma((put, 4))] * 5 + [dma((put, 2, 2))] + [dma((put,))] * 2 + [pltpu.SemaphoreType.REGULAR]
     results = pl.pallas_call(
         functools.partial(layer_kernel, get_table, put_table, widths),
@@ -1242,22 +1313,21 @@
         w_taps[0],
         gain_mixer,
         gain_mlp,
-        lengths,
+        lengths.T,
         dft,
         idft,
         *shards,
         hidden_in.reshape(tokens, features),
         out_grad.reshape(tokens, features),
     )
-    kinds = [(rows, 128), (3, rows), (1, rows), (1, rows)] + [(rows, width) for width in widths[1:]]
+    kinds = [(rows, 128), (3, 1, rows), (1, rows), (1, rows)] + [(rows, width) for width in widths[1:]]
     kinds = [jax.ShapeDtypeStruct(kind, f32) for kind in kinds] + kinds_of(results[5:])
     s_filters, s_taps, s_one, s_two, s_in, s_out, s_gu, s_dt, layer_out, input_grad = pl.pallas_call(
         finish_kernel,
         out_shape=kinds,
-        in_specs=[inside] * 5 + [anywhere] * 2,
-        out_specs=[inside] * 8 + [anywhere] * 2,
-        scratch_shapes=[dma((2,))],
-        compiler_params=pltpu.CompilerParams(vmem_limit_bytes=32 * 1024 * 1024),
+        in_specs=[inside] * 7,
+        out_specs=[inside] * 10,
+        compiler_params=pltpu.CompilerParams(vmem_limit_bytes=62 * 1024 * 1024),
     )(*results)
     shape = (1, micro, 1, slots, features)
     return (
@@ -1265,7 +1335,7 @@
         input_grad.reshape(shape),
         s_one,
         s_in[None],
-        s_taps[None],
+        s_taps.transpose(1, 0, 2),
         s_filters.T[None],
         s_out[None],
         s_two,

time: 262 us -> 233 us (0.89)
  Pallas kernels: 247 us -> 228 us
  local copies, waits for them, and re-layouts: 8.9 us -> 0 us
    pallas_call x1, Pallas kernels: 245 us -> 225 us  [fast_device(): pl.pallas_call(functools.partial(layer_kernel, get_table, put_table, widt...]
    unnamed x16 -> x0, local copies, waits for them, and re-layouts: 8.9 us -> none
where the time goes in v2:
time: 233 us; the launch traced here: 229 us
  Pallas kernels  228 us (98%)
    pallas_call x1, Pallas kernels, fast_device(): pl.pallas_call(functools.partial(layer_kernel, get_table, put_table, widt...  225 us

profile of v2, /device:TPU:28, one launch (start us, length us, event | category | flops | bytes accessed | tf_op | source)
XLA Modules:
  0.0 228.9 jit_solution(12491671116582229761)
XLA Ops:
  0.6 224.7 %shard_map.204 = (bf16[2,48,256]{2,1,0:T(8,128)(2,1)}, bf16[2,48,2304]{2,1,0:T(8,128)(2,1)}, bf16[2,48,768]{2,1,0:T(8,128)(2,1)}, bf16[2,48,6144]{2,1,0:T(8,128)...) custom-call(bf16[48,128]{1,0:T(8,128)(2,1)} %bitcast.35, ...), custom_call_target="tpu_custom_call" | custom-call | tf_op jit(solution)/shard_map/pallas_call | solution.py:1302
  225.3 3.6 %shard_map.205 = (f32[48,128]{1,0:T(8,128)}, f32[3,1,48]{2,1,0:T(1,128)}, f32[1,48]{1,0:T(1,128)}, f32[1,48]{1,0:T(1,128)}, f32[48,2304]{1,0:T(8,128)}, /*index=...) custom-call(bf16[2,48,256]{2,1,0:T(8,128)(2,1)} %get-tuple-element.2, ...), custom_call_target="tpu_custom_call" | custom-call | tf_op jit(solution)/shard_map/pallas_call | solution.py:1325
